TPU v7x, 512 devices: a whole 4x8x8 slice. The times are simulated.
512 devices in a mesh: rep: 32 (over y_lo, z), fsdp: 16 (over y_hi, x, core).
Axes of the slice: x: 4, y: 8 (y_hi: 2, y_lo: 4; y = y_hi * 4 + y_lo), z: 8, core: 2. Of those that a mesh axis runs over, the one named last changes fastest.
Arguments:
- activations: bfloat16 [32, 3072, 4096], P('rep', 'fsdp'), may hold values from -6 to 6
- cotangent: bfloat16 [32, 3072, 2048], P('rep', 'fsdp'), may hold values from -6 to 6
- local_weights: bfloat16 [32, 4096, 2048], P('rep', 'fsdp'), may hold values from -3 to 3
- base_shard: float32 [16, 256, 2048], P('fsdp', 'rep'), may hold values from -6 to 6
- momentum: float32 [16, 256, 2048], P('fsdp', 'rep'), may hold values from -3 to 3
Outputs:
- new_base: float32 [16, 256, 2048], P('fsdp', 'rep')
- new_moment: float32 [16, 256, 2048], P('fsdp', 'rep')
All inputs are finite; a program needn't handle non-finite values.
Results may differ from a plain program's by a relative error of at most 0.0095.
Values may be sent and summed in bfloat16 or wider, within the bound.
No kernel may reach another device: no remote copies, remote signals or barrier semaphores. Data moves between devices by JAX's collectives and lax.ppermute only.
A program may use at most 64 MiB of HBM per device.

v0:
```python
import math

import jax
import jax.numpy as jnp
from jax import lax
from jax.sharding import PartitionSpec as P

MOMENTUM_RATE = 0.9
OUTER_RATE = 0.7
EPSILON = 1e-06
TWO_PI = 2.0 * math.pi


def quantize(pseudo_grad):
    height, width = pseudo_grad.shape
    blocks = pseudo_grad.reshape(height, width // 128, 128)
    block_scale = (jnp.max(jnp.abs(blocks), axis=2) + EPSILON).astype(jnp.bfloat16)
    held_scale = lax.optimization_barrier(block_scale)
    level = 7.0 * (blocks / held_scale.astype(jnp.float32)[:, :, None])
    stair = level - jnp.sin(TWO_PI * level) / TWO_PI
    code_values = stair.astype(jnp.bfloat16)
    return (code_values, block_scale)


def restore(code_values, block_scale):
    return code_values.astype(jnp.float32) * (block_scale.astype(jnp.float32) / 7.0)[..., None]


def body(activations, cotangent, local_weights, base_shard, momentum):
    feature_block = lax.all_to_all(activations, "fsdp", split_axis=2, concat_axis=1, tiled=True)[0]
    total_rows = feature_block.shape[0]
    gradient = lax.dot_general(
        feature_block,
        lax.all_gather(cotangent, "fsdp", axis=1, tiled=True)[0],
        (((0,), (0,)), ((), ())),
        preferred_element_type=jnp.float32,
    )
    whole_base = lax.all_gather(base_shard, "rep", axis=1, tiled=True)[0]
    pseudo_grad = whole_base - (
        local_weights[0].astype(jnp.float32) - gradient * (1.0 / math.sqrt(total_rows))
    )
    code_values, block_scale = quantize(pseudo_grad)
    replicas = lax.axis_size("rep")
    share = pseudo_grad.shape[0] // replicas
    restored = restore(code_values, block_scale).reshape(pseudo_grad.shape)
    summed = lax.psum(restored, "rep")
    summed = lax.dynamic_slice_in_dim(summed, lax.axis_index("rep") * share, share, 0)
    average = (summed / replicas)[None]
    new_moment = MOMENTUM_RATE * momentum + average
    new_base = base_shard - OUTER_RATE * (average + MOMENTUM_RATE * new_moment)
    return (new_base, new_moment)


def solution(mesh):
    return jax.shard_map(
        body,
        mesh=mesh,
        in_specs=(
            P("rep", "fsdp", None),
            P("rep", "fsdp", None),
            P("rep", "fsdp", None),
            P("fsdp", "rep", None),
            P("fsdp", "rep", None),
        ),
        out_specs=(P("fsdp", "rep", None), P("fsdp", "rep", None)),
        check_vma=False,
    )
```

profile of v0, /device:TPU:4, one launch (start us, length us, event | category | flops | bytes accessed | tf_op | source)
XLA Modules:
  0.0 665.2 jit_solution(13211273311044773131)
XLA Ops:
  7.2 0.7 all-gather.3.cloned.1.call-update
  7.9 0.7 all-gather.5.cloned.1.call-update
  8.7 9.9 %copy.16 = bf16[1,192,4096]{1,0,2:T(2,128)(2,1)} copy(bf16[1,192,4096]{2,1,0:T(8,128)(2,1)} %param.5) | data formatting | bytes 3145728 | tf_op args[0]
  18.6 0.5 broadcast.30
  19.1 23.6 %reduce = bf16[4096,192]{1,0:T(8,128)(2,1)S(1)} reduce(bf16[4096,1,192]{2,1,0:T(2,128)(2,1)} %bitcast.47, bf16[]{:T(256)} %broadcast.30), dimensions={1}, to_apply=%bitcast.42.reduce_sub_computation | reduce | bytes 3145730
  42.8 3.3 reshape.20
  46.0 43.7 %all_to_all.15 = bf16[16,2,24576]{2,1,0:T(2,128)(2,1)S(1)} all-to-all(bf16[16,2,24576]{2,1,0:T(2,128)(2,1)} %reshape.20), channel_id=1, replica_groups=mesh['rep'=32,'fsdp'=16] {'fsdp'}, dimensions={0} | all-to-all | bytes 3145728 | tf_op jit(solution)/shard_map/all_to_all | solution.py:30
  89.7 7.3 %reshape.21 = bf16[4096,1,192]{2,1,0:T(2,128)(2,1)} reshape(bf16[16,2,24576]{2,1,0:T(2,128)(2,1)S(1)} %all_to_all.15) | data formatting | bytes 3145728
  97.0 9.9 %copy.17 = bf16[1,192,4096]{2,1,0:T(8,128)(2,1)S(1)} copy(bf16[1,192,4096]{1,0,2:T(2,128)(2,1)} %bitcast.48) | data formatting | bytes 3145728 | tf_op jit(solution)/shard_map/all_to_all | solution.py:30
  106.9 0.4 copy.22
  107.4 0.1 bitcast_bitcast_fusion
  107.5 1.8 copy.18
  109.2 71.9 %all-gather.3.cloned.1.call-done = f32[1,256,2048]{2,1,0:T(8,128)} async-done(((f32[1,8,2048]{2,1,0:T(8,128)}), f32[1,256,2048]{2,1,0:T(8,128)}) %all-gather.3.cloned.1.call-update) | async-done | bytes 2097168 | tf_op jit(solution)/shard_map/all_gather | solution.py:38
  181.1 142.9 %all-gather.5.cloned.1.call-done = bf16[1,3072,2048]{2,1,0:T(8,128)(2,1)} async-done(((bf16[1,192,2048]{2,1,0:T(8,128)(2,1)}), bf16[1,3072,2048]{2,1,0:T(8,128)(2,1)}) %all-gather.5.cloned.1.call-update) | async-done | bytes 12582928 | tf_op jit(solution)/shard_map/all_gather | solution.py:34
  324.0 9.1 %fusion.8 = f32[256,2048]{1,0:T(8,128)S(1)} fusion(bf16[3072,256]{1,0:T(8,128)(2,1)} %bitcast.52, bf16[1,3072,2048]{2,1,0:T(8,128)(2,1)} %all-gather.5.cloned.1.call-done, f32[1,256,2048]{2,1,0:T(8,128)} %all-gather.3.cloned.1.call-done, bf16[1,256,2048]{2,1,0:T(8,128)(2,1)S(1)} %copy-done), kind=kOutput, calls=%fused_computation.4 | convolution fusion | flops 3223322624 | bytes 19398656 | tf_op jit(solution)/shard_map/dot_general | solution.py:32
  333.1 0.2 abs_bitcast_fusion
  333.3 1.7 copy.23
  335.0 2.2 reduce_max.9
  337.3 0.1 copy.21
  337.5 0.6 mul.51
  338.1 0.6 div.26
  338.7 8.5 %bitcast_multiply_fusion = f32[256,2048]{1,0:T(8,128)} fusion(f32[32,8,16,128]{3,2,1,0:T(8,128)S(1)} %bitcast.50, f32[256,2048]{1,0:T(8,128)S(1)} %fusion.8, f32[32,8,16,128]{3,2,1,0:T(8,128)S(1)} %bitcast.51), kind=kLoop, calls=%fused_computation.5 | loop fusion | flops 4194304 | bytes 8388608 | tf_op jit(solution)/shard_map/mul | solution.py:26
  347.2 309.9 %all-reduce.2.cloned.1.call-done = f32[256,2048]{1,0:T(8,128)} async-done(((f32[256,2048]{1,0:T(8,128)}), f32[256,2048]{1,0:T(8,128)}) %all-reduce.2.cloned.1.call-update) | async-done | bytes 2097168 | tf_op jit(solution)/shard_map/psum | solution.py:46
  657.1 1.5 fusion.12
  (13 shorter events, 0.3 us)
Async XLA Ops:
  7.2 174.0 %all-gather.3.cloned.1.call-start = ((), (), s32[]{:S(2)}) async-start(), calls=%async_computation.1 | async-start | bytes 2162688 | tf_op jit(solution)/shard_map/all_gather | solution.py:38
  7.9 316.1 %all-gather.5.cloned.1.call-start = ((), (), s32[]{:S(2)}) async-start(), calls=%async_computation.2 | async-start | bytes 13369344 | tf_op jit(solution)/shard_map/all_gather | solution.py:34
  8.6 648.5 %all-reduce.2.cloned.1.call-start = ((), (), s32[]{:S(2)}) async-start(), calls=%async_computation.3 | async-start | bytes 4194304 | tf_op jit(solution)/shard_map/psum | solution.py:46
  107.5 216.5 %copy-start = (bf16[1,256,2048]{2,1,0:T(8,128)(2,1)S(1)}, bf16[1,256,2048]{2,1,0:T(8,128)(2,1)}, u32[]{:S(2)}) copy-start(bf16[1,256,2048]{2,1,0:T(8,128)(2,1)} %param.7) | copy-start | bytes 3145732
  347.2 309.9 %copy-start.1 = (f32[1,8,2048]{2,1,0:T(8,128)S(1)}, f32[1,8,2048]{2,1,0:T(8,128)}, u32[]{:S(2)}) copy-start(f32[1,8,2048]{2,1,0:T(8,128)} %param.8) | copy-start | bytes 196612
  347.2 309.9 %copy-start.2 = (f32[1,8,2048]{2,1,0:T(8,128)S(1)}, f32[1,8,2048]{2,1,0:T(8,128)}, u32[]{:S(2)}) copy-start(f32[1,8,2048]{2,1,0:T(8,128)} %param.9) | copy-start | bytes 196612
Sparse Core Ops, SparseCore 0:
  10.1 170.9 all-gather.2
  184.4 139.5 all-gather.4
  347.4 309.7 all-reduce.1
where the time goes:
time: 666 us; the launch traced here: 665 us
  waiting for transfers between devices  526 us (79%)
  blocking collectives  43.7 us (7%)
  local copies, waits for them, and re-layouts  36.3 us (5%)
  other arithmetic  36.1 us (5%)
  between operations  13.8 us (2%)
  matrix products  9.07 us (1%)
    psum x1, waiting for transfers between devices, body(): summed = lax.psum(restored, 'rep')  310 us
    all_gather x1, waiting for transfers between devices, body(): lax.all_gather(cotangent, 'fsdp', axis=1, tiled=True)[0]  143 us
    all_gather x1, waiting for transfers between devices, body(): whole_base = lax.all_gather(base_shard, 'rep', axis=1, tiled=True)[0]  71.9 us
    all_to_all x1, blocking collectives, body(): lax.all_to_all(activations, 'fsdp', split_axis=2, concat_axis=1, tiled=True)  43.7 us
    unnamed x2, other arithmetic  23.8 us
    unnamed x12, local copies, waits for them, and re-layouts  23.1 us
  transfers between devices with their start and end apart: 3, of which 3 were waited for; matrix products, arithmetic and copies ran while one was open for 9% of the time, Pallas kernels for 0%

commit v1 on v0

v1 whole, which is shorter than its diff:
```python
import math

import jax
import jax.numpy as jnp
from jax import lax
from jax.experimental import pallas as pl
from jax.experimental.pallas import tpu as pltpu
from jax.sharding import Mesh, PartitionSpec as P

MOMENTUM_RATE = 0.9
OUTER_RATE = 0.7
EPSILON = 1e-06
SINE = (6.57973575592041, -12.987845420837402, 12.207462310791016, -6.687273025512695, 2.36698842048645, -0.5099183320999146)
REP = ("ylo", "z")
PEERS = ("ylo", "z", "c")
X, YLO, Z = 4, 4, 8
N_REP = YLO * Z
TOK, D, W2 = 192, 4096, 2048
HALF = W2 // 2
ROWS = 512
INV = 1.0 / math.sqrt(TOK * 16)


def shift(size, k):
    return [(i, (i + k) % size) for i in range(size)]


def matmul_kernel(*refs):
    a_refs, c_refs, out_ref, a_all, c_all, sems = refs[:8], refs[8:12], refs[12], refs[13], refs[14], refs[15]
    copies = []
    for k in range(X):
        copies.append(pltpu.make_async_copy(c_refs[k], c_all.at[pl.ds(k * 384, 384)], sems.at[k]))
        copies.append(pltpu.make_async_copy(a_refs[k], a_all.at[pl.ds(k * 384, 192)], sems.at[4 + k]))
        copies.append(pltpu.make_async_copy(a_refs[4 + k], a_all.at[pl.ds(k * 384 + 192, 192)], sems.at[8 + k]))
    for c in copies:
        c.start()
    for c in copies:
        c.wait()
    for m in range(2):
        part = lax.dot_general(
            a_all[:, m * 256:(m + 1) * 256], c_all[...], (((0,), (0,)), ((), ())),
            preferred_element_type=jnp.float32)
        out_ref[m * 256:(m + 1) * 256, :] = (part * INV).astype(out_ref.dtype)


def matmul(a, c, dtype):
    return pl.pallas_call(
        matmul_kernel,
        out_shape=jax.ShapeDtypeStruct((ROWS, HALF), dtype),
        in_specs=[pl.BlockSpec(memory_space=pl.ANY)] * 12,
        out_specs=pl.BlockSpec(memory_space=pltpu.VMEM),
        scratch_shapes=[
            pltpu.VMEM((1536, ROWS), jnp.bfloat16),
            pltpu.VMEM((1536, HALF), jnp.bfloat16),
            pltpu.SemaphoreType.DMA((12,)),
        ],
        compiler_params=pltpu.CompilerParams(vmem_limit_bytes=40 * 1024 * 1024),
        cost_estimate=pl.CostEstimate(flops=2 * 1536 * ROWS * HALF, bytes_accessed=7 << 20, transcendentals=0),
    )(*a, *c)


def quantize_kernel(own_ref, part_ref, local_ref, base_ref, out_ref):
    rows = own_ref.shape[0]
    pairs = rows // 8
    for j in range(0, 8, 2):
        restored = []
        for col in (j, j + 1):
            lanes = slice(col * 128, (col + 1) * 128)
            gradient = own_ref[:, lanes] + part_ref[:, lanes].astype(jnp.float32)
            base = base_ref[:, 0, col * 8:(col + 1) * 8, :].reshape(rows, 128)
            pseudo = base - (local_ref[:, lanes].astype(jnp.float32) - gradient)
            scale = (jnp.max(jnp.abs(pseudo), axis=1, keepdims=True) + EPSILON).astype(jnp.bfloat16).astype(jnp.float32)
            level = pseudo * (7.0 / scale)
            step = jnp.round(level)
            off = level - step
            square = off * off
            poly = SINE[-1]
            for coef in SINE[-2::-1]:
                poly = poly * square + coef
            code = (step + off * square * poly).astype(jnp.bfloat16).astype(jnp.float32)
            restored.append((code * (scale * (1.0 / 7.0))).reshape(pairs, 8, 128))
        out_ref[:, 0, j * 8:(j + 2) * 8, :] = jnp.concatenate(restored, axis=1).astype(jnp.bfloat16)


def quantize(own, part, local, base):
    rows = 64
    steps = 256 // rows
    tile = pl.BlockSpec((rows, HALF), lambda c, i: (c * steps + i, 0))
    blocks = pl.BlockSpec((rows // 8, 1, 64, 128), lambda c, i: (i, c, 0, 0))
    return pl.pallas_call(
        quantize_kernel,
        grid=(2, steps),
        out_shape=jax.ShapeDtypeStruct((N_REP, 2, 64, 128), jnp.bfloat16),
        in_specs=[tile, tile, tile, blocks],
        out_specs=blocks,
        compiler_params=pltpu.CompilerParams(vmem_limit_bytes=32 * 1024 * 1024),
        cost_estimate=pl.CostEstimate(flops=30 * ROWS * HALF, bytes_accessed=6 << 20, transcendentals=0),
    )(own, part, local, base)


def outer_kernel(got_ref, base_ref, moment_ref, new_base_ref, new_moment_ref):
    for c in range(2):
        total = jnp.sum(got_ref[:, c].astype(jnp.float32), axis=0)
        for j in range(8):
            lanes = slice(c * HALF + j * 128, c * HALF + (j + 1) * 128)
            average = total[j * 8:(j + 1) * 8] / N_REP
            moment = MOMENTUM_RATE * moment_ref[:, lanes] + average
            new_moment_ref[:, lanes] = moment
            new_base_ref[:, lanes] = base_ref[:, lanes] - OUTER_RATE * (average + MOMENTUM_RATE * moment)


def outer(got, base, moment):
    shape = jax.ShapeDtypeStruct(base.shape, jnp.float32)
    return pl.pallas_call(
        outer_kernel,
        out_shape=(shape, shape),
        compiler_params=pltpu.CompilerParams(vmem_limit_bytes=32 * 1024 * 1024),
        cost_estimate=pl.CostEstimate(flops=2 << 20, bytes_accessed=2 << 20, transcendentals=0),
    )(got, base, moment)


def body(activations, cotangent, local_weights, base_shard, momentum):
    x, yhi, c = lax.axis_index("x"), lax.axis_index("yhi"), lax.axis_index("c")
    act, cot, local, base, moment = activations[0], cotangent[0], local_weights[0], base_shard[0], momentum[0]

    def columns(array, index, width):
        return lax.dynamic_slice_in_dim(array, index * width, width, 1)

    def other_core(array):
        return lax.ppermute(array, "c", shift(2, 1))

    mine = columns(cot, c, HALF)
    pair = jnp.concatenate([mine, other_core(columns(cot, 1 - c, HALF))])
    c_parts = [pair] + [lax.ppermute(pair, "x", shift(X, k)) for k in range(1, X)]

    def features(half):
        own = [columns(act, half * X + lax.rem(x + k, X), ROWS) for k in range(X)]
        own = [own[0]] + [lax.ppermute(own[k], "x", shift(X, k)) for k in range(1, X)]
        return own + [other_core(a) for a in own]

    far = matmul(features(1 - yhi), c_parts, jnp.bfloat16)
    far = lax.ppermute(far, "yhi", shift(2, 1))
    near = matmul(features(yhi), c_parts, jnp.float32)

    local_mine, local_other = columns(local, c, HALF), other_core(columns(local, 1 - c, HALF))
    local_rows = jnp.concatenate([jnp.where(c == 0, local_mine, local_other), jnp.where(c == 0, local_other, local_mine)])

    sent = base.reshape(8, 2, 8, 128).transpose(1, 2, 0, 3).reshape(2, 64, 128)
    sent = jnp.broadcast_to(sent[None], (N_REP, 2, 64, 128)).reshape(2 * N_REP, 64, 128)
    base_rows = lax.all_to_all(sent, PEERS, 0, 0, tiled=True).reshape(N_REP, 2, 64, 128)

    restored = quantize(near, far, local_rows, base_rows)
    got = lax.all_to_all(restored.reshape(2 * N_REP, 64, 128), PEERS, 0, 0, tiled=True)
    new_base, new_moment = outer(got.reshape(N_REP, 2, 64, 128), base, moment)
    return new_base[None], new_moment[None]


def solution(mesh):
    fine = Mesh(mesh.devices.reshape(YLO, Z, 2, X, 2), ("ylo", "z", "yhi", "x", "c"))
    rep, fsdp = REP, ("yhi", "x", "c")
    return jax.shard_map(
        body,
        mesh=fine,
        in_specs=(
            P(rep, fsdp, None),
            P(rep, fsdp, None),
            P(rep, fsdp, None),
            P(fsdp, rep, None),
            P(fsdp, rep, None),
        ),
        out_specs=(P(fsdp, rep, None), P(fsdp, rep, None)),
        check_vma=False,
    )
```

time: 666 us -> 194 us (0.29)
  the two profiles are of different devices: /device:TPU:4 before, /device:TPU:1 now
where the time goes in v1:
time: 194 us; the launch traced here: 193 us
  starting transfers between devices  72.5 us (37%)
  blocking collectives  57.6 us (30%)
  waiting for transfers between devices  34.8 us (18%)
  Pallas kernels  15.8 us (8%)
  local copies, waits for them, and re-layouts  9.6 us (5%)
    all_to_all x1, blocking collectives, body(): lax.all_to_all(restored.reshape(2 * N_REP, 64, 128), PEERS, 0, 0, tiled=T...  57.6 us
    ppermute x6, waiting for transfers between devices, features(): lax.ppermute(own[k], 'x', shift(X, k))  34.6 us
    ppermute x10, starting transfers between devices, other_core(): return lax.ppermute(array, 'c', shift(2, 1))  24 us
    ppermute x6, starting transfers between devices, features(): lax.ppermute(own[k], 'x', shift(X, k))  18.5 us
    all_to_all x1, starting transfers between devices, body(): lax.all_to_all(sent, PEERS, 0, 0, tiled=True).reshape(N_REP, 2, 64, 128)  15.5 us
    ppermute x3, starting transfers between devices, body(): lax.ppermute(pair, 'x', shift(X, k))  9.64 us
    pallas_call x2, Pallas kernels, matmul(): pl.pallas_call(matmul_kernel, out_shape=jax.ShapeDtypeStruct((ROWS, HALF)...  9.55 us
    pallas_call x1, Pallas kernels, quantize(): pl.pallas_call(quantize_kernel, grid=(2, steps), out_shape=jax.ShapeDtype...  5.39 us
  transfers between devices with their start and end apart: 21, of which 3 were waited for; matrix products, arithmetic and copies ran while one was open for 3% of the time, Pallas kernels for 5%

profile of v1, /device:TPU:1, one launch (start us, length us, event | category | flops | bytes accessed | tf_op | source)
XLA Modules:
  0.0 192.8 jit_solution(15168654322337874647)
XLA Ops:
  0.6 2.5 %broadcast_in_dim.14 = f32[32,2,64,128]{3,2,1,0:T(8,128)} broadcast(f32[2,64,128]{2,1,0:T(8,128)} %bitcast.41), dimensions={1,2,3} | broadcast | bytes 2162688 | tf_op jit(solution)/shard_map/broadcast_in_dim | solution.py:149
  3.1 15.5 %all-to-all-start = ((f32[64,64,128]{2,1,0:T(8,128)}), f32[64,64,128]{2,1,0:T(8,128)S(1)}, u32[]{:S(2)}, u32[]{:S(2)}) async-start(f32[64,64,128]{2,1,0:T(8,128)} %bitcast.44), calls=%async_computation | async-start | bytes 4194304 | tf_op jit(solution)/shard_map/all_to_all | solution.py:150
  19.5 2.4 %collective-permute-start.7 = (bf16[192,1024]{1,0:T(8,128)(2,1)}, bf16[192,1024]{1,0:T(8,128)(2,1)S(1)}, u32[]{:S(2)}, u32[]{:S(2)}) collective-permute-start(bf16[192,1024]{1,0:T(8,128)(2,1)} %get-tuple-element.17), channel_id=1, source_target_pairs={{0,1},{1,0},{2,3},{3,2},{4,5},{5,4},{6,7},{7,6},{8,9},{9,8},{10,11... | collective-permute-start | bytes 1179656 | tf_op jit(solution)/shard_map/ppermute | solution.py:130
  21.9 2.5 %dynamic-slice_bitcast_fusion.3 = (bf16[192,512]{1,0:T(8,128)(2,1)S(1)}, bf16[192,512]{1,0:T(8,128)(2,1)S(1)}, bf16[192,512]{1,0:T(8,128)(2,1)S(1)}, bf16[192,51...) fusion(bf16[1,192,4096]{2,1,0:T(8,128)(2,1)} %param.5, ...), kind=kLoop, calls=%fused_computation.7 | loop fusion | bytes 3145760 | tf_op jit(solution)/shard_map/dynamic_slice | solution.py:127
  24.4 3.1 %collective-permute-start.11 = (bf16[192,512]{1,0:T(8,128)(2,1)S(1)}, bf16[192,512]{1,0:T(8,128)(2,1)S(1)}, u32[]{:S(2)}, u32[]{:S(2)}) collective-permute-start(bf16[192,512]{1,0:T(8,128)(2,1)S(1)} %get-tuple-element.9), channel_id=1, source_target_pairs={{0,2},{2,4},{4,6},{6,0},{1,3},{3,5},{5,7},{7,1},{8,10},{10,12},{12... | collective-permute-start | bytes 589832 | tf_op jit(solution)/shard_map/ppermute | solution.py:138
  27.6 3.4 %collective-permute-start.10 = (bf16[384,1024]{1,0:T(8,128)(2,1)S(1)}, bf16[384,1024]{1,0:T(8,128)(2,1)S(1)}, u32[]{:S(2)}, u32[]{:S(2)}) collective-permute-start(bf16[384,1024]{1,0:T(8,128)(2,1)S(1)} %pad_maximum_fusion.1.refs_8_), channel_id=1, source_target_pairs={{0,6},{2,0},{4,2},{6,4},{1,7},{3,1},{5,3},{7,5},{8,14},{10,8},{12,... | collective-permute-start | bytes 2359304 | tf_op jit(solution)/shard_map/ppermute | solution.py:134
  32.9 4.3 %collective-permute-start.9 = (bf16[384,1024]{1,0:T(8,128)(2,1)S(1)}, bf16[384,1024]{1,0:T(8,128)(2,1)S(1)}, u32[]{:S(2)}, u32[]{:S(2)}) collective-permute-start(bf16[384,1024]{1,0:T(8,128)(2,1)S(1)} %pad_maximum_fusion.1.refs_8_), channel_id=1, source_target_pairs={{0,4},{2,6},{4,0},{6,2},{1,5},{3,7},{5,1},{7,3},{8,12},{10,14},{12... | collective-permute-start | bytes 2359304 | tf_op jit(solution)/shard_map/ppermute | solution.py:134
  37.2 2.4 %collective-permute-start.12 = (bf16[192,512]{1,0:T(8,128)(2,1)S(1)}, bf16[192,512]{1,0:T(8,128)(2,1)S(1)}, u32[]{:S(2)}, u32[]{:S(2)}) collective-permute-start(bf16[192,512]{1,0:T(8,128)(2,1)S(1)} %get-tuple-element.15), channel_id=1, source_target_pairs={{0,4},{2,6},{4,0},{6,2},{1,5},{3,7},{5,1},{7,3},{8,12},{10,14},{12... | collective-permute-start | bytes 589832 | tf_op jit(solution)/shard_map/ppermute | solution.py:138
  39.7 4.6 %collective-permute-start.13 = (bf16[192,512]{1,0:T(8,128)(2,1)S(1)}, bf16[192,512]{1,0:T(8,128)(2,1)S(1)}, u32[]{:S(2)}, u32[]{:S(2)}) collective-permute-start(bf16[192,512]{1,0:T(8,128)(2,1)S(1)} %get-tuple-element.8), channel_id=1, source_target_pairs={{0,6},{2,0},{4,2},{6,4},{1,7},{3,1},{5,3},{7,5},{8,14},{10,8},{12,... | collective-permute-start | bytes 589832 | tf_op jit(solution)/shard_map/ppermute | solution.py:138
  44.3 29.1 %collective-permute-done.12.refs_2_ = bf16[192,512]{1,0:T(8,128)(2,1)S(1)} collective-permute-done((bf16[192,512]{1,0:T(8,128)(2,1)S(1)}, bf16[192,512]{1,0:T(8,128)(2,1)S(1)}, u32[]{:S(2)}, u32[]{:S(2)}) %collective-permute-start.12) | collective-permute-done | bytes 196640 | tf_op jit(solution)/shard_map/ppermute | solution.py:138
  73.4 3.4 %collective-permute-start.14 = (bf16[192,512]{1,0:T(8,128)(2,1)S(1)}, bf16[192,512]{1,0:T(8,128)(2,1)S(1)}, u32[]{:S(2)}, u32[]{:S(2)}) collective-permute-start(bf16[192,512]{1,0:T(8,128)(2,1)S(1)} %get-tuple-element.10.refs_0_), channel_id=1, source_target_pairs={{0,1},{1,0},{2,3},{3,2},{4,5},{5,4},{6,7},{7,6},{8,9},{9,8},{10,11... | collective-permute-start | bytes 589832 | tf_op jit(solution)/shard_map/ppermute | solution.py:130
  76.9 1.9 collective-permute-start.15
  78.8 2.4 %collective-permute-start.16 = (bf16[192,512]{1,0:T(8,128)(2,1)S(1)}, bf16[192,512]{1,0:T(8,128)(2,1)S(1)}, u32[]{:S(2)}, u32[]{:S(2)}) collective-permute-start(bf16[192,512]{1,0:T(8,128)(2,1)S(1)} %collective-permute-done.12.refs_2_), channel_id=1, source_target_pairs={{0,1},{1,0},{2,3},{3,2},{4,5},{5,4},{6,7},{7,6},{8,9},{9,8},{10,11... | collective-permute-start | bytes 589832 | tf_op jit(solution)/shard_map/ppermute | solution.py:130
  84.0 2.5 %collective-permute-start.19 = (bf16[256,1024]{1,0:T(8,128)(2,1)}, bf16[256,1024]{1,0:T(8,128)(2,1)}, u32[]{:S(2)}, u32[]{:S(2)}) collective-permute-start(bf16[256,1024]{1,0:T(8,128)(2,1)} %dynamic-slice_bitcast_fusion), channel_id=1, source_target_pairs={{0,1},{1,0},{2,3},{3,2},{4,5},{5,4},{6,7},{7,6},{8,9},{9,8},{10,11... | collective-permute-start | bytes 1572872 | tf_op jit(solution)/shard_map/ppermute | solution.py:130
  86.7 5.2 %shard_map.69 = bf16[512,1024]{1,0:T(8,128)(2,1)} custom-call(bf16[192,512]{1,0:T(8,128)(2,1)S(1)} %get-tuple-element.10.refs_0_, bf16[192,512]{1,0:T(8,128)(2,1)S(1)} %collective-permute-done.11.refs_1_, bf16[192,512]{1,0:T(8,128)(2,1)S(1)} %collective-permute-done.12.refs_2_, bf16[192,512]{1,0:T(8,128)(2,1)S(1)} %collective-permute-done.13.refs_3_, ...), custom_call_target="tpu_custom_call" | custom-call | flops 1610612736 | bytes 7340032 | tf_op jit(solution)/shard_map/pallas_call | solution.py:47
  91.9 4.8 %collective-permute-start.18 = (bf16[512,1024]{1,0:T(8,128)(2,1)}, bf16[512,1024]{1,0:T(8,128)(2,1)}, u32[]{:S(2)}, u32[]{:S(2)}) collective-permute-start(bf16[512,1024]{1,0:T(8,128)(2,1)} %shard_map.69), channel_id=1, source_target_pairs={{0,8},{8,0},{1,9},{9,1},{2,10},{10,2},{3,11},{11,3},{4,12},{12,4},... | collective-permute-start | bytes 3145736 | tf_op jit(solution)/shard_map/ppermute | solution.py:142
  98.6 3.1 %collective-permute-start.1 = (bf16[192,512]{1,0:T(8,128)(2,1)}, bf16[192,512]{1,0:T(8,128)(2,1)}, u32[]{:S(2)}, u32[]{:S(2)}) collective-permute-start(bf16[192,512]{1,0:T(8,128)(2,1)} %get-tuple-element.12), channel_id=1, source_target_pairs={{0,4},{2,6},{4,0},{6,2},{1,5},{3,7},{5,1},{7,3},{8,12},{10,14},{12... | collective-permute-start | bytes 589832 | tf_op jit(solution)/shard_map/ppermute | solution.py:138
  101.7 3.4 %collective-permute-start.2 = (bf16[192,512]{1,0:T(8,128)(2,1)}, bf16[192,512]{1,0:T(8,128)(2,1)}, u32[]{:S(2)}, u32[]{:S(2)}) collective-permute-start(bf16[192,512]{1,0:T(8,128)(2,1)} %get-tuple-element.11), channel_id=1, source_target_pairs={{0,6},{2,0},{4,2},{6,4},{1,7},{3,1},{5,3},{7,5},{8,14},{10,8},{12,... | collective-permute-start | bytes 589832 | tf_op jit(solution)/shard_map/ppermute | solution.py:138
  105.1 5.4 %collective-permute-done.refs_1_ = bf16[192,512]{1,0:T(8,128)(2,1)S(1)} collective-permute-done((bf16[192,512]{1,0:T(8,128)(2,1)}, bf16[192,512]{1,0:T(8,128)(2,1)S(1)}, u32[]{:S(2)}, u32[]{:S(2)}) %collective-permute-start) | collective-permute-done | bytes 196640 | tf_op jit(solution)/shard_map/ppermute | solution.py:138
  110.5 3.2 %collective-permute-start.3 = (bf16[192,512]{1,0:T(8,128)(2,1)S(1)}, bf16[192,512]{1,0:T(8,128)(2,1)S(1)}, u32[]{:S(2)}, u32[]{:S(2)}) collective-permute-start(bf16[192,512]{1,0:T(8,128)(2,1)S(1)} %get-tuple-element.14.refs_0_), channel_id=1, source_target_pairs={{0,1},{1,0},{2,3},{3,2},{4,5},{5,4},{6,7},{7,6},{8,9},{9,8},{10,11... | collective-permute-start | bytes 589832 | tf_op jit(solution)/shard_map/ppermute | solution.py:130
  115.6 2.4 %collective-permute-start.5 = (bf16[192,512]{1,0:T(8,128)(2,1)}, bf16[192,512]{1,0:T(8,128)(2,1)S(1)}, u32[]{:S(2)}, u32[]{:S(2)}) collective-permute-start(bf16[192,512]{1,0:T(8,128)(2,1)} %collective-permute-done.1.refs_2_), channel_id=1, source_target_pairs={{0,1},{1,0},{2,3},{3,2},{4,5},{5,4},{6,7},{7,6},{8,9},{9,8},{10,11... | collective-permute-start | bytes 589832 | tf_op jit(solution)/shard_map/ppermute | solution.py:130
  121.6 4.4 %shard_map.68.own_ref = f32[512,1024]{1,0:T(8,128)S(1)} custom-call(bf16[192,512]{1,0:T(8,128)(2,1)S(1)} %get-tuple-element.14.refs_0_, bf16[192,512]{1,0:T(8,128)(2,1)S(1)} %collective-permute-done.refs_1_, bf16[192,512]{1,0:T(8,128)(2,1)} %collective-permute-done.1.refs_2_, bf16[192,512]{1,0:T(8,128)(2,1)} %collective-permute-done.2.refs_3_, ...), custom_call_target="tpu_custom_call" | custom-call | flops 1610612736 | bytes 7340032 | tf_op jit(solution)/shard_map/pallas_call | solution.py:47
  128.9 5.4 %shard_map.70 = bf16[32,2,64,128]{3,2,1,0:T(8,128)(2,1)S(1)} custom-call(f32[512,1024]{1,0:T(8,128)S(1)} %copy-done.1, bf16[512,1024]{1,0:T(8,128)(2,1)} %collective-permute-done.18.part_ref, bf16[512,1024]{1,0:T(8,128)(2,1)S(1)} %pad_maximum_fusion.local_ref, f32[32,2,64,128]{3,2,1,0:T(8,128)S(1)} %bitcast.38), custom_call_target="tpu_custom_call" | custom-call | flops 15728640 | bytes 6291456 | tf_op jit(solution)/shard_map/pallas_call | solution.py:90
  134.4 57.6 %all_to_all.10 = bf16[64,64,128]{2,1,0:T(8,128)(2,1)S(1)} all-to-all(bf16[64,64,128]{2,1,0:T(8,128)(2,1)S(1)} %bitcast.39), channel_id=1, replica_groups=mesh['ylo'=4,'z'=8,'yhi'=2,'x'=4,'c'=2] {'ylo','z','c'}, dimensions={0} | all-to-all | bytes 2097152 | tf_op jit(solution)/shard_map/all_to_all | solution.py:153
  (60 shorter events, 16.8 us)
Async XLA Ops:
  3.1 124.3 %all-to-all-start = ((f32[64,64,128]{2,1,0:T(8,128)}), f32[64,64,128]{2,1,0:T(8,128)S(1)}, u32[]{:S(2)}, u32[]{:S(2)}) async-start(f32[64,64,128]{2,1,0:T(8,128)} %bitcast.44), calls=%async_computation | async-start | bytes 4194304 | tf_op jit(solution)/shard_map/all_to_all | solution.py:150
  19.5 8.0 %collective-permute-start.7 = (bf16[192,1024]{1,0:T(8,128)(2,1)}, bf16[192,1024]{1,0:T(8,128)(2,1)S(1)}, u32[]{:S(2)}, u32[]{:S(2)}) collective-permute-start(bf16[192,1024]{1,0:T(8,128)(2,1)} %get-tuple-element.17), channel_id=1, source_target_pairs={{0,1},{1,0},{2,3},{3,2},{4,5},{5,4},{6,7},{7,6},{8,9},{9,8},{10,11... | collective-permute-start | bytes 1179656 | tf_op jit(solution)/shard_map/ppermute | solution.py:130
  21.9 61.3 %copy-start.12 = (bf16[1,256,2048]{2,1,0:T(8,128)(2,1)S(1)}, bf16[1,256,2048]{2,1,0:T(8,128)(2,1)}, u32[]{:S(2)}) copy-start(bf16[1,256,2048]{2,1,0:T(8,128)(2,1)} %param.7) | copy-start | bytes 3145732
  24.4 15.3 %collective-permute-start.11 = (bf16[192,512]{1,0:T(8,128)(2,1)S(1)}, bf16[192,512]{1,0:T(8,128)(2,1)S(1)}, u32[]{:S(2)}, u32[]{:S(2)}) collective-permute-start(bf16[192,512]{1,0:T(8,128)(2,1)S(1)} %get-tuple-element.9), channel_id=1, source_target_pairs={{0,2},{2,4},{4,6},{6,0},{1,3},{3,5},{5,7},{7,1},{8,10},{10,12},{12... | collective-permute-start | bytes 589832 | tf_op jit(solution)/shard_map/ppermute | solution.py:138
  27.6 64.3 %copy-start.2 = (bf16[384,1024]{1,0:T(8,128)(2,1)}, bf16[384,1024]{1,0:T(8,128)(2,1)S(1)}, u32[]{:S(2)}) copy-start(bf16[384,1024]{1,0:T(8,128)(2,1)S(1)} %pad_maximum_fusion.1.refs_8_) | copy-start | bytes 2359300
  27.6 59.0 %collective-permute-start.10 = (bf16[384,1024]{1,0:T(8,128)(2,1)S(1)}, bf16[384,1024]{1,0:T(8,128)(2,1)S(1)}, u32[]{:S(2)}, u32[]{:S(2)}) collective-permute-start(bf16[384,1024]{1,0:T(8,128)(2,1)S(1)} %pad_maximum_fusion.1.refs_8_), channel_id=1, source_target_pairs={{0,6},{2,0},{4,2},{6,4},{1,7},{3,1},{5,3},{7,5},{8,14},{10,8},{12,... | collective-permute-start | bytes 2359304 | tf_op jit(solution)/shard_map/ppermute | solution.py:134
  31.0 55.7 %collective-permute-start.8 = (bf16[384,1024]{1,0:T(8,128)(2,1)S(1)}, bf16[384,1024]{1,0:T(8,128)(2,1)S(1)}, u32[]{:S(2)}, u32[]{:S(2)}) collective-permute-start(bf16[384,1024]{1,0:T(8,128)(2,1)S(1)} %pad_maximum_fusion.1.refs_8_), channel_id=1, source_target_pairs={{0,2},{2,4},{4,6},{6,0},{1,3},{3,5},{5,7},{7,1},{8,10},{10,12},{12... | collective-permute-start | bytes 2359304 | tf_op jit(solution)/shard_map/ppermute | solution.py:134
  32.9 53.8 %collective-permute-start.9 = (bf16[384,1024]{1,0:T(8,128)(2,1)S(1)}, bf16[384,1024]{1,0:T(8,128)(2,1)S(1)}, u32[]{:S(2)}, u32[]{:S(2)}) collective-permute-start(bf16[384,1024]{1,0:T(8,128)(2,1)S(1)} %pad_maximum_fusion.1.refs_8_), channel_id=1, source_target_pairs={{0,4},{2,6},{4,0},{6,2},{1,5},{3,7},{5,1},{7,3},{8,12},{10,14},{12... | collective-permute-start | bytes 2359304 | tf_op jit(solution)/shard_map/ppermute | solution.py:134
  37.2 36.2 %collective-permute-start.12 = (bf16[192,512]{1,0:T(8,128)(2,1)S(1)}, bf16[192,512]{1,0:T(8,128)(2,1)S(1)}, u32[]{:S(2)}, u32[]{:S(2)}) collective-permute-start(bf16[192,512]{1,0:T(8,128)(2,1)S(1)} %get-tuple-element.15), channel_id=1, source_target_pairs={{0,4},{2,6},{4,0},{6,2},{1,5},{3,7},{5,1},{7,3},{8,12},{10,14},{12... | collective-permute-start | bytes 589832 | tf_op jit(solution)/shard_map/ppermute | solution.py:138
  39.7 37.2 %collective-permute-start.13 = (bf16[192,512]{1,0:T(8,128)(2,1)S(1)}, bf16[192,512]{1,0:T(8,128)(2,1)S(1)}, u32[]{:S(2)}, u32[]{:S(2)}) collective-permute-start(bf16[192,512]{1,0:T(8,128)(2,1)S(1)} %get-tuple-element.8), channel_id=1, source_target_pairs={{0,6},{2,0},{4,2},{6,4},{1,7},{3,1},{5,3},{7,5},{8,14},{10,8},{12,... | collective-permute-start | bytes 589832 | tf_op jit(solution)/shard_map/ppermute | solution.py:138
  73.4 5.4 %collective-permute-start.14 = (bf16[192,512]{1,0:T(8,128)(2,1)S(1)}, bf16[192,512]{1,0:T(8,128)(2,1)S(1)}, u32[]{:S(2)}, u32[]{:S(2)}) collective-permute-start(bf16[192,512]{1,0:T(8,128)(2,1)S(1)} %get-tuple-element.10.refs_0_), channel_id=1, source_target_pairs={{0,1},{1,0},{2,3},{3,2},{4,5},{5,4},{6,7},{7,6},{8,9},{9,8},{10,11... | collective-permute-start | bytes 589832 | tf_op jit(solution)/shard_map/ppermute | solution.py:130
  76.9 4.4 %collective-permute-start.15 = (bf16[192,512]{1,0:T(8,128)(2,1)S(1)}, bf16[192,512]{1,0:T(8,128)(2,1)S(1)}, u32[]{:S(2)}, u32[]{:S(2)}) collective-permute-start(bf16[192,512]{1,0:T(8,128)(2,1)S(1)} %collective-permute-done.11.refs_1_), channel_id=1, source_target_pairs={{0,1},{1,0},{2,3},{3,2},{4,5},{5,4},{6,7},{7,6},{8,9},{9,8},{10,11... | collective-permute-start | bytes 589832 | tf_op jit(solution)/shard_map/ppermute | solution.py:130
  78.8 5.2 %collective-permute-start.16 = (bf16[192,512]{1,0:T(8,128)(2,1)S(1)}, bf16[192,512]{1,0:T(8,128)(2,1)S(1)}, u32[]{:S(2)}, u32[]{:S(2)}) collective-permute-start(bf16[192,512]{1,0:T(8,128)(2,1)S(1)} %collective-permute-done.12.refs_2_), channel_id=1, source_target_pairs={{0,1},{1,0},{2,3},{3,2},{4,5},{5,4},{6,7},{7,6},{8,9},{9,8},{10,11... | collective-permute-start | bytes 589832 | tf_op jit(solution)/shard_map/ppermute | solution.py:130
  81.2 5.4 %collective-permute-start.17 = (bf16[192,512]{1,0:T(8,128)(2,1)S(1)}, bf16[192,512]{1,0:T(8,128)(2,1)S(1)}, u32[]{:S(2)}, u32[]{:S(2)}) collective-permute-start(bf16[192,512]{1,0:T(8,128)(2,1)S(1)} %collective-permute-done.13.refs_3_), channel_id=1, source_target_pairs={{0,1},{1,0},{2,3},{3,2},{4,5},{5,4},{6,7},{7,6},{8,9},{9,8},{10,11... | collective-permute-start | bytes 589832 | tf_op jit(solution)/shard_map/ppermute | solution.py:130
  84.0 34.0 %collective-permute-start.19 = (bf16[256,1024]{1,0:T(8,128)(2,1)}, bf16[256,1024]{1,0:T(8,128)(2,1)}, u32[]{:S(2)}, u32[]{:S(2)}) collective-permute-start(bf16[256,1024]{1,0:T(8,128)(2,1)} %dynamic-slice_bitcast_fusion), channel_id=1, source_target_pairs={{0,1},{1,0},{2,3},{3,2},{4,5},{5,4},{6,7},{7,6},{8,9},{9,8},{10,11... | collective-permute-start | bytes 1572872 | tf_op jit(solution)/shard_map/ppermute | solution.py:130
  91.9 35.5 %collective-permute-start.18 = (bf16[512,1024]{1,0:T(8,128)(2,1)}, bf16[512,1024]{1,0:T(8,128)(2,1)}, u32[]{:S(2)}, u32[]{:S(2)}) collective-permute-start(bf16[512,1024]{1,0:T(8,128)(2,1)} %shard_map.69), channel_id=1, source_target_pairs={{0,8},{8,0},{1,9},{9,1},{2,10},{10,2},{3,11},{11,3},{4,12},{12,4},... | collective-permute-start | bytes 3145736 | tf_op jit(solution)/shard_map/ppermute | solution.py:142
  96.7 13.8 %collective-permute-start = (bf16[192,512]{1,0:T(8,128)(2,1)}, bf16[192,512]{1,0:T(8,128)(2,1)S(1)}, u32[]{:S(2)}, u32[]{:S(2)}) collective-permute-start(bf16[192,512]{1,0:T(8,128)(2,1)} %get-tuple-element.13), channel_id=1, source_target_pairs={{0,2},{2,4},{4,6},{6,0},{1,3},{3,5},{5,7},{7,1},{8,10},{10,12},{12... | collective-permute-start | bytes 589832 | tf_op jit(solution)/shard_map/ppermute | solution.py:138
  98.6 15.1 %collective-permute-start.1 = (bf16[192,512]{1,0:T(8,128)(2,1)}, bf16[192,512]{1,0:T(8,128)(2,1)}, u32[]{:S(2)}, u32[]{:S(2)}) collective-permute-start(bf16[192,512]{1,0:T(8,128)(2,1)} %get-tuple-element.12), channel_id=1, source_target_pairs={{0,4},{2,6},{4,0},{6,2},{1,5},{3,7},{5,1},{7,3},{8,12},{10,14},{12... | collective-permute-start | bytes 589832 | tf_op jit(solution)/shard_map/ppermute | solution.py:138
  101.7 14.0 %collective-permute-start.2 = (bf16[192,512]{1,0:T(8,128)(2,1)}, bf16[192,512]{1,0:T(8,128)(2,1)}, u32[]{:S(2)}, u32[]{:S(2)}) collective-permute-start(bf16[192,512]{1,0:T(8,128)(2,1)} %get-tuple-element.11), channel_id=1, source_target_pairs={{0,6},{2,0},{4,2},{6,4},{1,7},{3,1},{5,3},{7,5},{8,14},{10,8},{12,... | collective-permute-start | bytes 589832 | tf_op jit(solution)/shard_map/ppermute | solution.py:138
  110.5 10.9 %collective-permute-start.3 = (bf16[192,512]{1,0:T(8,128)(2,1)S(1)}, bf16[192,512]{1,0:T(8,128)(2,1)S(1)}, u32[]{:S(2)}, u32[]{:S(2)}) collective-permute-start(bf16[192,512]{1,0:T(8,128)(2,1)S(1)} %get-tuple-element.14.refs_0_), channel_id=1, source_target_pairs={{0,1},{1,0},{2,3},{3,2},{4,5},{5,4},{6,7},{7,6},{8,9},{9,8},{10,11... | collective-permute-start | bytes 589832 | tf_op jit(solution)/shard_map/ppermute | solution.py:130
  113.7 7.7 %collective-permute-start.4 = (bf16[192,512]{1,0:T(8,128)(2,1)S(1)}, bf16[192,512]{1,0:T(8,128)(2,1)S(1)}, u32[]{:S(2)}, u32[]{:S(2)}) collective-permute-start(bf16[192,512]{1,0:T(8,128)(2,1)S(1)} %collective-permute-done.refs_1_), channel_id=1, source_target_pairs={{0,1},{1,0},{2,3},{3,2},{4,5},{5,4},{6,7},{7,6},{8,9},{9,8},{10,11... | collective-permute-start | bytes 589832 | tf_op jit(solution)/shard_map/ppermute | solution.py:130
  115.6 5.8 %collective-permute-start.5 = (bf16[192,512]{1,0:T(8,128)(2,1)}, bf16[192,512]{1,0:T(8,128)(2,1)S(1)}, u32[]{:S(2)}, u32[]{:S(2)}) collective-permute-start(bf16[192,512]{1,0:T(8,128)(2,1)} %collective-permute-done.1.refs_2_), channel_id=1, source_target_pairs={{0,1},{1,0},{2,3},{3,2},{4,5},{5,4},{6,7},{7,6},{8,9},{9,8},{10,11... | collective-permute-start | bytes 589832 | tf_op jit(solution)/shard_map/ppermute | solution.py:130
  118.1 3.5 %collective-permute-start.6 = (bf16[192,512]{1,0:T(8,128)(2,1)}, bf16[192,512]{1,0:T(8,128)(2,1)S(1)}, u32[]{:S(2)}, u32[]{:S(2)}) collective-permute-start(bf16[192,512]{1,0:T(8,128)(2,1)} %collective-permute-done.2.refs_3_), channel_id=1, source_target_pairs={{0,1},{1,0},{2,3},{3,2},{4,5},{5,4},{6,7},{7,6},{8,9},{9,8},{10,11... | collective-permute-start | bytes 589832 | tf_op jit(solution)/shard_map/ppermute | solution.py:130
  134.4 57.6 %copy-start.10 = (f32[1,8,2048]{2,1,0:T(8,128)S(1)}, f32[1,8,2048]{2,1,0:T(8,128)}, u32[]{:S(2)}) copy-start(f32[1,8,2048]{2,1,0:T(8,128)} %param.8) | copy-start | bytes 196612
  (12 other events, 172.3 us)

commit v2 on v1

v2 whole, which is shorter than its diff:
```python
import math

import jax
import jax.numpy as jnp
from jax import lax
from jax.experimental import pallas as pl
from jax.experimental.pallas import tpu as pltpu
from jax.sharding import Mesh, PartitionSpec as P

MOMENTUM_RATE = 0.9
OUTER_RATE = 0.7
EPSILON = 1e-06
SINE = (6.57973575592041, -12.987845420837402, 12.207462310791016, -6.687273025512695, 2.36698842048645, -0.5099183320999146)
COST = pl.CostEstimate(flops=1, bytes_accessed=1, transcendentals=0)
REP = ("ylo", "z")
PEERS = ("ylo", "z", "c")
X, YLO, Z = 4, 4, 8
N_REP = YLO * Z
TOK, D, W2 = 192, 4096, 2048
HALF = W2 // 2
CHUNK = HALF // 2
BLOCKS = CHUNK // 128
ROWS = 512
INV = 1.0 / math.sqrt(TOK * 16)


def shift(size, k):
    return [(i, (i + k) % size) for i in range(size)]


def matmul_kernel(*refs):
    others, features, columns, out_ref = refs[:X], refs[X:2 * X], refs[2 * X:3 * X], refs[3 * X]
    a_all, c_all, sems = refs[3 * X + 1:]
    copies = []
    for k in range(X):
        copies.append((others[k], a_all.at[k, 1]))
        copies.append((features[k].at[0], a_all.at[k, 0]))
        copies.append((columns[k].at[1:3], c_all.at[k]))
    copies = [pltpu.make_async_copy(*ends, sems.at[i]) for i, ends in enumerate(copies)]
    for copy in copies:
        copy.start()
    for copy in copies:
        copy.wait()
    everything = c_all[...].reshape(2 * X * TOK, CHUNK)
    for m in range(2):
        rows = slice(m * 256, (m + 1) * 256)
        part = lax.dot_general(
            a_all[:, :, :, rows].reshape(2 * X * TOK, 256), everything, (((0,), (0,)), ((), ())),
            preferred_element_type=jnp.float32)
        out_ref[rows, :] = (part * INV).astype(out_ref.dtype)


def matmul(others, features, columns, dtype):
    return pl.pallas_call(
        matmul_kernel,
        out_shape=jax.ShapeDtypeStruct((ROWS, CHUNK), dtype),
        in_specs=[pl.BlockSpec(memory_space=pl.ANY)] * (3 * X),
        out_specs=pl.BlockSpec(memory_space=pltpu.VMEM),
        scratch_shapes=[
            pltpu.VMEM((X, 2, TOK, ROWS), jnp.bfloat16),
            pltpu.VMEM((X, 2, TOK, CHUNK), jnp.bfloat16),
            pltpu.SemaphoreType.DMA((3 * X,)),
        ],
        compiler_params=pltpu.CompilerParams(vmem_limit_bytes=8 * 1024 * 1024),
        cost_estimate=COST,
    )(*others, *features, *columns)


def quantize_kernel(own_ref, part_ref, local_ref, base_ref, out_ref):
    rows = own_ref.shape[0]
    for j in range(0, BLOCKS, 2):
        restored = []
        for col in (j, j + 1):
            lanes = slice(col * 128, (col + 1) * 128)
            gradient = own_ref[:, lanes] + part_ref[:, lanes].astype(jnp.float32)
            base = base_ref[0, :, 0, :, lanes].reshape(rows, 128)
            pseudo = base - (local_ref[:, lanes].astype(jnp.float32) - gradient)
            scale = (jnp.max(jnp.abs(pseudo), axis=1, keepdims=True) + EPSILON).astype(jnp.bfloat16).astype(jnp.float32)
            level = pseudo * (7.0 / scale)
            step = jnp.round(level)
            off = level - step
            square = off * off
            poly = SINE[-1]
            for coef in SINE[-2::-1]:
                poly = poly * square + coef
            code = (step + off * square * poly).astype(jnp.bfloat16).astype(jnp.float32)
            restored.append((code * (scale * (1.0 / 7.0))).reshape(Z, 8, 128))
        block = jnp.concatenate(restored, axis=1).astype(jnp.bfloat16)
        out_ref[0, :, 0, j * 8:(j + 2) * 8, :] = block


def quantize(own, part, local, base, chunk, earlier=None):
    rows = 8 * Z
    tile = pl.BlockSpec((rows, CHUNK), lambda c, i: (c * YLO + i, 0))
    local_tile = pl.BlockSpec((rows, CHUNK), lambda c, i: (c * YLO + i, chunk))
    out_tile = pl.BlockSpec((1, Z, 1, BLOCKS * 8, 128), lambda c, i: (i, 0, c, chunk, 0))
    base_tile = pl.BlockSpec((1, Z, 1, 8, CHUNK), lambda c, i: (i, 0, c, 0, chunk))
    operands, specs, kernel, aliases = [own, part, local, base], [tile, tile, local_tile, base_tile], quantize_kernel, {}
    if earlier is not None:
        operands.append(earlier)
        specs.append(pl.BlockSpec(memory_space=pl.ANY))
        kernel, aliases = (lambda *refs: quantize_kernel(*refs[:4], refs[5])), {4: 0}
    return pl.pallas_call(
        kernel,
        grid=(2, YLO),
        out_shape=jax.ShapeDtypeStruct((YLO, Z, 2, 2 * BLOCKS * 8, 128), jnp.bfloat16),
        in_specs=specs,
        out_specs=out_tile,
        input_output_aliases=aliases,
        compiler_params=pltpu.CompilerParams(vmem_limit_bytes=5 * 1024 * 1024),
        cost_estimate=COST,
    )(*operands)


def outer_kernel(got_ref, base_ref, moment_ref, new_base_ref, new_moment_ref):
    for c in range(2):
        total = jnp.sum(got_ref[:, c].astype(jnp.float32), axis=0)
        for j in range(2 * BLOCKS):
            lanes = slice(c * HALF + j * 128, c * HALF + (j + 1) * 128)
            average = total[j * 8:(j + 1) * 8] / N_REP
            moment = MOMENTUM_RATE * moment_ref[:, lanes] + average
            new_moment_ref[:, lanes] = moment
            new_base_ref[:, lanes] = base_ref[:, lanes] - OUTER_RATE * (average + MOMENTUM_RATE * moment)


def outer(got, base, moment):
    shape = jax.ShapeDtypeStruct(base.shape, jnp.float32)
    return pl.pallas_call(
        outer_kernel,
        out_shape=(shape, shape),
        compiler_params=pltpu.CompilerParams(vmem_limit_bytes=8 * 1024 * 1024),
        cost_estimate=COST,
    )(got, base, moment)


def body(activations, cotangent, local_weights, base_shard, momentum):
    x, yhi, c = lax.axis_index("x"), lax.axis_index("yhi"), lax.axis_index("c")
    act, cot, local, base, moment = activations[0], cotangent[0], local_weights[0], base_shard[0], momentum[0]

    def columns(array, start, width):
        return lax.dynamic_slice_in_dim(array, start, width, 1)

    def other_core(array):
        return lax.ppermute(array, "c", shift(2, 1))

    def along_x(array, k):
        return lax.ppermute(array, "x", shift(X, k))

    def all_to_all(array, axes):
        return lax.all_to_all(array, axes, 0, 0, tiled=True)

    def after(array, *others):
        return lax.optimization_barrier((array, *others))[0]

    cot_mine, cot_other = columns(cot, c * HALF, HALF), other_core(columns(cot, (1 - c) * HALF, HALF))

    def group(j, half):
        chunk = slice(j * CHUNK, (j + 1) * CHUNK)

        def packed(k):
            return jnp.stack([columns(act, (half * X + lax.rem(x + k, X)) * ROWS, ROWS), cot_mine[:, chunk], cot_other[:, chunk]])

        return [packed(0)] + [along_x(packed(k), k) for k in range(1, X)]

    def other_features(parts):
        return [other_core(part[0]) for part in parts]

    groups = [group(0, 1 - yhi), group(1, yhi)]
    far_other = other_features(groups[0])
    sent_far = [matmul(far_other, groups[0], groups[0], jnp.bfloat16)]
    groups[1] = after(groups[1], sent_far[0])
    sent_far.append(matmul(far_other, groups[0], groups[1], jnp.bfloat16))
    far = [lax.ppermute(part, "yhi", shift(2, 1)) for part in sent_far]
    near_other = other_features(after(groups[1], sent_far[1]))
    near = [matmul(near_other, groups[1], groups[j], jnp.float32) for j in range(2)]
    far[0] = after(far[0], *near)

    local = after(local, sent_far[1])
    local_mine, local_other = columns(local, c * HALF, HALF), other_core(columns(local, (1 - c) * HALF, HALF))
    local_rows = jnp.concatenate([jnp.where(c == 0, local_mine, local_other), jnp.where(c == 0, local_other, local_mine)])

    sent = base.reshape(8, 2, HALF).transpose(1, 0, 2)
    sent = jnp.broadcast_to(sent[None], (N_REP, 2, 8, HALF)).reshape(2 * N_REP, 8, HALF)
    base_rows = all_to_all(sent, PEERS).reshape(YLO, Z, 2, 8, HALF)

    restored = quantize(near[0], far[0], local_rows, base_rows, 0)
    restored = quantize(near[1], far[1], local_rows, base_rows, 1, restored)
    got = all_to_all(restored.reshape(2 * N_REP, 64, 128), PEERS).reshape(N_REP, 2, 64, 128)
    new_base, new_moment = outer(got, base, moment)
    return new_base[None], new_moment[None]


def solution(mesh):
    fine = Mesh(mesh.devices.reshape(YLO, Z, 2, X, 2), ("ylo", "z", "yhi", "x", "c"))
    rep, fsdp = REP, ("yhi", "x", "c")
    return jax.shard_map(
        body,
        mesh=fine,
        in_specs=(
            P(rep, fsdp, None),
            P(rep, fsdp, None),
            P(rep, fsdp, None),
            P(fsdp, rep, None),
            P(fsdp, rep, None),
        ),
        out_specs=(P(fsdp, rep, None), P(fsdp, rep, None)),
        check_vma=False,
    )
```

time: 194 us -> 177 us (0.912)
  waiting for transfers between devices: 34.8 us -> 14.7 us
  blocking collectives: 57.6 us -> 43.4 us
  Pallas kernels: 15.8 us -> 26.2 us
  local copies, waits for them, and re-layouts: 9.6 us -> 17.5 us
  starting transfers between devices: 72.5 us -> 70.4 us
    ppermute x10 -> x8, waiting for transfers between devices: 34.6 us -> 13.7 us  [the longest x6 13.7 us: along_x(): return lax.ppermute(array, 'x', shift(X, k))]
    all_to_all x1, blocking collectives: 57.6 us -> 43.4 us  [all_to_all(): return lax.all_to_all(array, axes, 0, 0, tiled=True)]
    pallas_call x3 -> x6, Pallas kernels: 14.9 us -> 25.4 us  [the longest x4 16.1 us: matmul(): pl.pallas_call(matmul_kernel, out_shape=jax.ShapeDtypeStruct((ROWS, CHUNK...]
    unnamed x30 -> x46, local copies, waits for them, and re-layouts: 2.98 us -> 10.2 us
    ppermute x10 -> x8, starting transfers between devices: 32.9 us -> 30.1 us  [the longest x6 20.6 us: along_x(): return lax.ppermute(array, 'x', shift(X, k))]
  transfers between devices with their start and end apart: 21 -> 19, of which waited for: 3 -> 4; matrix products, arithmetic and copies ran while one was open for 3% -> 4% of each run, Pallas kernels for 5% -> 12%
where the time goes in v2:
time: 177 us; the launch traced here: 175 us
  starting transfers between devices  70.4 us (40%)
  blocking collectives  43.4 us (25%)
  Pallas kernels  26.2 us (15%)
  local copies, waits for them, and re-layouts  17.5 us (10%)
  waiting for transfers between devices  14.7 us (8%)
  other arithmetic  1.78 us (1%)
    all_to_all x1, blocking collectives, all_to_all(): return lax.all_to_all(array, axes, 0, 0, tiled=True)  43.4 us
    ppermute x10, starting transfers between devices, other_core(): return lax.ppermute(array, 'c', shift(2, 1))  24.7 us
    ppermute x6, starting transfers between devices, along_x(): return lax.ppermute(array, 'x', shift(X, k))  20.6 us
    pallas_call x4, Pallas kernels, matmul(): pl.pallas_call(matmul_kernel, out_shape=jax.ShapeDtypeStruct((ROWS, CHUNK...  16.1 us
    all_to_all x1, starting transfers between devices, all_to_all(): return lax.all_to_all(array, axes, 0, 0, tiled=True)  15.5 us
    ppermute x6, waiting for transfers between devices, along_x(): return lax.ppermute(array, 'x', shift(X, k))  13.7 us
    unnamed x46, local copies, waits for them, and re-layouts  10.2 us
    ppermute x2, starting transfers between devices, body(): far = [lax.ppermute(part, 'yhi', shift(2, 1)) for part in sent_far]  9.49 us
  transfers between devices with their start and end apart: 19, of which 4 were waited for; matrix products, arithmetic and copies ran while one was open for 4% of the time, Pallas kernels for 12%

profile of v2, /device:TPU:1, one launch (start us, length us, event | category | flops | bytes accessed | tf_op | source)
XLA Modules:
  0.0 175.3 jit_solution(4578952520315512814)
XLA Ops:
  0.6 2.4 %broadcast_in_dim.12 = f32[32,2,8,1024]{3,2,1,0:T(8,128)} broadcast(f32[2,8,1024]{2,1,0:T(8,128)} %bitcast.43), dimensions={1,2,3} | broadcast | bytes 2162688 | tf_op jit(solution)/shard_map/broadcast_in_dim | solution.py:183
  3.1 15.5 %all-to-all-start = ((f32[64,8,1024]{2,1,0:T(8,128)}), f32[64,8,1024]{2,1,0:T(8,128)S(1)}, u32[]{:S(2)}, u32[]{:S(2)}) async-start(f32[64,8,1024]{2,1,0:T(8,128)} %bitcast.46), calls=%async_computation | async-start | bytes 4194304 | tf_op jit(solution)/shard_map/all_to_all | solution.py:150
  23.8 4.7 %collective-permute-start.7 = (bf16[3,192,512]{2,1,0:T(8,128)(2,1)S(1)}, bf16[3,192,512]{2,1,0:T(8,128)(2,1)S(1)}, u32[]{:S(2)}, u32[]{:S(2)}) collective-permute-start(bf16[3,192,512]{2,1,0:T(8,128)(2,1)S(1)} %get-tuple-element.39), channel_id=1, source_target_pairs={{0,4},{2,6},{4,0},{6,2},{1,5},{3,7},{5,1},{7,3},{8,12},{10,14},{12... | collective-permute-start | bytes 1769480 | tf_op jit(solution)/shard_map/ppermute | solution.py:147
  28.4 2.8 %collective-permute-start.9 = (bf16[3,192,512]{2,1,0:T(8,128)(2,1)S(1)}, bf16[3,192,512]{2,1,0:T(8,128)(2,1)S(1)}, u32[]{:S(2)}, u32[]{:S(2)}) collective-permute-start(bf16[3,192,512]{2,1,0:T(8,128)(2,1)S(1)} %get-tuple-element.40), channel_id=1, source_target_pairs={{0,6},{2,0},{4,2},{6,4},{1,7},{3,1},{5,3},{7,5},{8,14},{10,8},{12,... | collective-permute-start | bytes 1769480 | tf_op jit(solution)/shard_map/ppermute | solution.py:147
  31.2 2.7 %collective-permute-start.4 = (bf16[192,512]{1,0:T(8,128)(2,1)S(1)}, bf16[192,512]{1,0:T(8,128)(2,1)S(1)}, u32[]{:S(2)}, u32[]{:S(2)}) collective-permute-start(bf16[192,512]{1,0:T(8,128)(2,1)S(1)} %bitcast.49), channel_id=1, source_target_pairs={{0,1},{1,0},{2,3},{3,2},{4,5},{5,4},{6,7},{7,6},{8,9},{9,8},{10,11... | collective-permute-start | bytes 589832 | tf_op jit(solution)/shard_map/ppermute | solution.py:144
  33.9 2.5 %collective-permute-start.5 = (bf16[3,192,512]{2,1,0:T(8,128)(2,1)S(1)}, bf16[3,192,512]{2,1,0:T(8,128)(2,1)S(1)}, u32[]{:S(2)}, u32[]{:S(2)}) collective-permute-start(bf16[3,192,512]{2,1,0:T(8,128)(2,1)S(1)} %get-tuple-element.41), channel_id=1, source_target_pairs={{0,2},{2,4},{4,6},{6,0},{1,3},{3,5},{5,7},{7,1},{8,10},{10,12},{12... | collective-permute-start | bytes 1769480 | tf_op jit(solution)/shard_map/ppermute | solution.py:147
  36.6 4.0 %collective-permute-start.3 = (bf16[3,192,512]{2,1,0:T(8,128)(2,1)S(1)}, bf16[3,192,512]{2,1,0:T(8,128)(2,1)S(1)}, u32[]{:S(2)}, u32[]{:S(2)}) collective-permute-start(bf16[3,192,512]{2,1,0:T(8,128)(2,1)S(1)} %get-tuple-element.46), channel_id=1, source_target_pairs={{0,6},{2,0},{4,2},{6,4},{1,7},{3,1},{5,3},{7,5},{8,14},{10,8},{12,... | collective-permute-start | bytes 1769480 | tf_op jit(solution)/shard_map/ppermute | solution.py:147
  41.9 3.1 %collective-permute-start.1 = (bf16[3,192,512]{2,1,0:T(8,128)(2,1)S(1)}, bf16[3,192,512]{2,1,0:T(8,128)(2,1)S(1)}, u32[]{:S(2)}, u32[]{:S(2)}) collective-permute-start(bf16[3,192,512]{2,1,0:T(8,128)(2,1)S(1)} %get-tuple-element.47), channel_id=1, source_target_pairs={{0,2},{2,4},{4,6},{6,0},{1,3},{3,5},{5,7},{7,1},{8,10},{10,12},{12... | collective-permute-start | bytes 1769480 | tf_op jit(solution)/shard_map/ppermute | solution.py:147
  45.1 9.6 %collective-permute-done.9.refs_7_.refs_11_ = bf16[3,192,512]{2,1,0:T(8,128)(2,1)S(1)} collective-permute-done((bf16[3,192,512]{2,1,0:T(8,128)(2,1)S(1)}, bf16[3,192,512]{2,1,0:T(8,128)(2,1)S(1)}, u32[]{:S(2)}, u32[]{:S(2)}) %collective-permute-start.9) | collective-permute-done | bytes 589856 | tf_op jit(solution)/shard_map/ppermute | solution.py:147
  54.7 3.6 %collective-permute-start.2 = (bf16[3,192,512]{2,1,0:T(8,128)(2,1)S(1)}, bf16[3,192,512]{2,1,0:T(8,128)(2,1)S(1)}, u32[]{:S(2)}, u32[]{:S(2)}) collective-permute-start(bf16[3,192,512]{2,1,0:T(8,128)(2,1)S(1)} %get-tuple-element.48), channel_id=1, source_target_pairs={{0,4},{2,6},{4,0},{6,2},{1,5},{3,7},{5,1},{7,3},{8,12},{10,14},{12... | collective-permute-start | bytes 1769480 | tf_op jit(solution)/shard_map/ppermute | solution.py:147
  58.3 3.8 %collective-permute-start.8 = (bf16[192,512]{1,0:T(8,128)(2,1)S(1)}, bf16[192,512]{1,0:T(8,128)(2,1)S(1)}, u32[]{:S(2)}, u32[]{:S(2)}) collective-permute-start(bf16[192,512]{1,0:T(8,128)(2,1)S(1)} %slice_bitcast_fusion.1), channel_id=1, source_target_pairs={{0,1},{1,0},{2,3},{3,2},{4,5},{5,4},{6,7},{7,6},{8,9},{9,8},{10,11... | collective-permute-start | bytes 589832 | tf_op jit(solution)/shard_map/ppermute | solution.py:144
  64.1 2.4 %collective-permute-start.6 = (bf16[192,512]{1,0:T(8,128)(2,1)S(1)}, bf16[192,512]{1,0:T(8,128)(2,1)S(1)}, u32[]{:S(2)}, u32[]{:S(2)}) collective-permute-start(bf16[192,512]{1,0:T(8,128)(2,1)S(1)} %slice_bitcast_fusion.2), channel_id=1, source_target_pairs={{0,1},{1,0},{2,3},{3,2},{4,5},{5,4},{6,7},{7,6},{8,9},{9,8},{10,11... | collective-permute-start | bytes 589832 | tf_op jit(solution)/shard_map/ppermute | solution.py:144
  67.6 4.7 %shard_map.68 = bf16[512,512]{1,0:T(8,128)(2,1)} custom-call(bf16[192,512]{1,0:T(8,128)(2,1)S(1)} %collective-permute-done.4.refs_0_, bf16[192,512]{1,0:T(8,128)(2,1)S(1)} %collective-permute-done.6.refs_1_, bf16[192,512]{1,0:T(8,128)(2,1)S(1)} %collective-permute-done.8.refs_2_, bf16[192,512]{1,0:T(8,128)(2,1)S(1)} %collective-permute-done.10.refs_3_, ...), custom_call_target="tpu_custom_call" | custom-call | flops 1 | bytes 1 | tf_op jit(solution)/shard_map/pallas_call | solution.py:54
  72.3 4.8 %collective-permute-start.17 = (bf16[512,512]{1,0:T(8,128)(2,1)}, bf16[512,512]{1,0:T(8,128)(2,1)}, u32[]{:S(2)}, u32[]{:S(2)}) collective-permute-start(bf16[512,512]{1,0:T(8,128)(2,1)} %shard_map.68), channel_id=1, source_target_pairs={{0,8},{8,0},{1,9},{9,1},{2,10},{10,2},{3,11},{11,3},{4,12},{12,4},... | collective-permute-start | bytes 1572872 | tf_op jit(solution)/shard_map/ppermute | solution.py:173
  77.1 2.8 %collective-permute-done.2.refs_10_.refs_6_ = bf16[3,192,512]{2,1,0:T(8,128)(2,1)S(1)} collective-permute-done((bf16[3,192,512]{2,1,0:T(8,128)(2,1)S(1)}, bf16[3,192,512]{2,1,0:T(8,128)(2,1)S(1)}, u32[]{:S(2)}, u32[]{:S(2)}) %collective-permute-start.2) | collective-permute-done | bytes 589856 | tf_op jit(solution)/shard_map/ppermute | solution.py:147
  79.9 4.7 %shard_map.69 = bf16[512,512]{1,0:T(8,128)(2,1)} custom-call(bf16[192,512]{1,0:T(8,128)(2,1)S(1)} %collective-permute-done.4.refs_0_, bf16[192,512]{1,0:T(8,128)(2,1)S(1)} %collective-permute-done.6.refs_1_, bf16[192,512]{1,0:T(8,128)(2,1)S(1)} %collective-permute-done.8.refs_2_, bf16[192,512]{1,0:T(8,128)(2,1)S(1)} %collective-permute-done.10.refs_3_, ...), custom_call_target="tpu_custom_call" | custom-call | flops 1 | bytes 1 | tf_op jit(solution)/shard_map/pallas_call | solution.py:54
  85.5 2.9 %collective-permute-start.16 = (bf16[256,1024]{1,0:T(8,128)(2,1)}, bf16[256,1024]{1,0:T(8,128)(2,1)}, u32[]{:S(2)}, u32[]{:S(2)}) collective-permute-start(bf16[256,1024]{1,0:T(8,128)(2,1)} %constant_dynamic-slice_fusion), channel_id=1, source_target_pairs={{0,1},{1,0},{2,3},{3,2},{4,5},{5,4},{6,7},{7,6},{8,9},{9,8},{10,11... | collective-permute-start | bytes 1572872 | tf_op jit(solution)/shard_map/ppermute | solution.py:144
  91.1 2.4 %collective-permute-start.13 = (bf16[192,512]{1,0:T(8,128)(2,1)S(1)}, bf16[192,512]{1,0:T(8,128)(2,1)S(1)}, u32[]{:S(2)}, u32[]{:S(2)}) collective-permute-start(bf16[192,512]{1,0:T(8,128)(2,1)S(1)} %slice_bitcast_fusion.8), channel_id=1, source_target_pairs={{0,1},{1,0},{2,3},{3,2},{4,5},{5,4},{6,7},{7,6},{8,9},{9,8},{10,11... | collective-permute-start | bytes 589832 | tf_op jit(solution)/shard_map/ppermute | solution.py:144
  99.3 4.7 %collective-permute-start.15 = (bf16[512,512]{1,0:T(8,128)(2,1)}, bf16[512,512]{1,0:T(8,128)(2,1)}, u32[]{:S(2)}, u32[]{:S(2)}) collective-permute-start(bf16[512,512]{1,0:T(8,128)(2,1)} %shard_map.69), channel_id=1, source_target_pairs={{0,8},{8,0},{1,9},{9,1},{2,10},{10,2},{3,11},{11,3},{4,12},{12,4},... | collective-permute-start | bytes 1572872 | tf_op jit(solution)/shard_map/ppermute | solution.py:173
  111.3 3.4 %shard_map.71.own_ref = f32[512,512]{1,0:T(8,128)S(1)} custom-call(bf16[192,512]{1,0:T(8,128)(2,1)} %collective-permute-done.11.refs_0_, bf16[192,512]{1,0:T(8,128)(2,1)} %collective-permute-done.12.refs_1_, bf16[192,512]{1,0:T(8,128)(2,1)S(1)} %copy-done.17, bf16[192,512]{1,0:T(8,128)(2,1)S(1)} %collective-permute-done.14.refs_3_, ...), custom_call_target="tpu_custom_call" | custom-call | flops 1 | bytes 1 | tf_op jit(solution)/shard_map/pallas_call | solution.py:54
  114.7 3.4 %shard_map.70.refs_0_ = f32[512,512]{1,0:T(8,128)S(1)} custom-call(bf16[192,512]{1,0:T(8,128)(2,1)} %collective-permute-done.11.refs_0_, bf16[192,512]{1,0:T(8,128)(2,1)} %collective-permute-done.12.refs_1_, bf16[192,512]{1,0:T(8,128)(2,1)S(1)} %copy-done.17, bf16[192,512]{1,0:T(8,128)(2,1)S(1)} %collective-permute-done.14.refs_3_, ...), custom_call_target="tpu_custom_call" | custom-call | flops 1 | bytes 1 | tf_op jit(solution)/shard_map/pallas_call | solution.py:54
  121.7 4.7 %shard_map.72.refs_4_ = bf16[4,8,2,64,128]{4,3,2,1,0:T(8,128)(2,1)S(1)} custom-call(f32[512,512]{1,0:T(8,128)S(1)} %copy-done.15, bf16[512,512]{1,0:T(8,128)(2,1)} %collective-permute-done.17.part_ref, bf16[512,1024]{1,0:T(8,128)(2,1)S(1)} %pad_maximum_fusion.local_ref.refs_2_, f32[4,8,2,8,1024]{4,3,2,1,0:T(8,128)S(1)} %bitcast.39), custom_call_target="tpu_custom_call" | custom-call | flops 1 | bytes 1 | tf_op jit(solution)/shard_map/pallas_call | solution.py:103
  126.4 4.6 %shard_map.73 = bf16[4,8,2,64,128]{4,3,2,1,0:T(8,128)(2,1)S(1)} custom-call(f32[512,512]{1,0:T(8,128)S(1)} %copy-done.13, bf16[512,512]{1,0:T(8,128)(2,1)} %collective-permute-done.15.refs_1_, bf16[512,1024]{1,0:T(8,128)(2,1)S(1)} %pad_maximum_fusion.local_ref.refs_2_, f32[4,8,2,8,1024]{4,3,2,1,0:T(8,128)S(1)} %bitcast.40, ...), custom_call_target="tpu_custom_call", output_to_operand_aliasing={{}: (4, {})} | custom-call | flops 1 | bytes 1 | tf_op jit(solution)/shard_map/pallas_call | solution.py:103
  131.0 43.4 %all_to_all.10 = bf16[64,64,128]{2,1,0:T(8,128)(2,1)S(1)} all-to-all(bf16[64,64,128]{2,1,0:T(8,128)(2,1)S(1)} %bitcast.41), channel_id=1, replica_groups=mesh['ylo'=4,'z'=8,'yhi'=2,'x'=4,'c'=2] {'ylo','z','c'}, dimensions={0} | all-to-all | bytes 2097152 | tf_op jit(solution)/shard_map/all_to_all | solution.py:150
  (85 shorter events, 30.5 us)
Async XLA Ops:
  3.1 117.4 %all-to-all-start = ((f32[64,8,1024]{2,1,0:T(8,128)}), f32[64,8,1024]{2,1,0:T(8,128)S(1)}, u32[]{:S(2)}, u32[]{:S(2)}) async-start(f32[64,8,1024]{2,1,0:T(8,128)} %bitcast.46), calls=%async_computation | async-start | bytes 4194304 | tf_op jit(solution)/shard_map/all_to_all | solution.py:150
  19.5 4.0 %collective-permute-start = (bf16[192,1024]{1,0:T(8,128)(2,1)}, bf16[192,1024]{1,0:T(8,128)(2,1)S(1)}, u32[]{:S(2)}, u32[]{:S(2)}) collective-permute-start(bf16[192,1024]{1,0:T(8,128)(2,1)} %get-tuple-element.37), channel_id=1, source_target_pairs={{0,1},{1,0},{2,3},{3,2},{4,5},{5,4},{6,7},{7,6},{8,9},{9,8},{10,11... | collective-permute-start | bytes 1179656 | tf_op jit(solution)/shard_map/ppermute | solution.py:144
  23.8 18.2 %collective-permute-start.7 = (bf16[3,192,512]{2,1,0:T(8,128)(2,1)S(1)}, bf16[3,192,512]{2,1,0:T(8,128)(2,1)S(1)}, u32[]{:S(2)}, u32[]{:S(2)}) collective-permute-start(bf16[3,192,512]{2,1,0:T(8,128)(2,1)S(1)} %get-tuple-element.39), channel_id=1, source_target_pairs={{0,4},{2,6},{4,0},{6,2},{1,5},{3,7},{5,1},{7,3},{8,12},{10,14},{12... | collective-permute-start | bytes 1769480 | tf_op jit(solution)/shard_map/ppermute | solution.py:147
  28.4 26.2 %collective-permute-start.9 = (bf16[3,192,512]{2,1,0:T(8,128)(2,1)S(1)}, bf16[3,192,512]{2,1,0:T(8,128)(2,1)S(1)}, u32[]{:S(2)}, u32[]{:S(2)}) collective-permute-start(bf16[3,192,512]{2,1,0:T(8,128)(2,1)S(1)} %get-tuple-element.40), channel_id=1, source_target_pairs={{0,6},{2,0},{4,2},{6,4},{1,7},{3,1},{5,3},{7,5},{8,14},{10,8},{12,... | collective-permute-start | bytes 1769480 | tf_op jit(solution)/shard_map/ppermute | solution.py:147
  31.2 31.0 %collective-permute-start.4 = (bf16[192,512]{1,0:T(8,128)(2,1)S(1)}, bf16[192,512]{1,0:T(8,128)(2,1)S(1)}, u32[]{:S(2)}, u32[]{:S(2)}) collective-permute-start(bf16[192,512]{1,0:T(8,128)(2,1)S(1)} %bitcast.49), channel_id=1, source_target_pairs={{0,1},{1,0},{2,3},{3,2},{4,5},{5,4},{6,7},{7,6},{8,9},{9,8},{10,11... | collective-permute-start | bytes 589832 | tf_op jit(solution)/shard_map/ppermute | solution.py:144
  33.9 24.4 %collective-permute-start.5 = (bf16[3,192,512]{2,1,0:T(8,128)(2,1)S(1)}, bf16[3,192,512]{2,1,0:T(8,128)(2,1)S(1)}, u32[]{:S(2)}, u32[]{:S(2)}) collective-permute-start(bf16[3,192,512]{2,1,0:T(8,128)(2,1)S(1)} %get-tuple-element.41), channel_id=1, source_target_pairs={{0,2},{2,4},{4,6},{6,0},{1,3},{3,5},{5,7},{7,1},{8,10},{10,12},{12... | collective-permute-start | bytes 1769480 | tf_op jit(solution)/shard_map/ppermute | solution.py:147
  36.6 40.4 %collective-permute-start.3 = (bf16[3,192,512]{2,1,0:T(8,128)(2,1)S(1)}, bf16[3,192,512]{2,1,0:T(8,128)(2,1)S(1)}, u32[]{:S(2)}, u32[]{:S(2)}) collective-permute-start(bf16[3,192,512]{2,1,0:T(8,128)(2,1)S(1)} %get-tuple-element.46), channel_id=1, source_target_pairs={{0,6},{2,0},{4,2},{6,4},{1,7},{3,1},{5,3},{7,5},{8,14},{10,8},{12,... | collective-permute-start | bytes 1769480 | tf_op jit(solution)/shard_map/ppermute | solution.py:147
  41.9 37.9 %copy-start = (bf16[3,192,512]{2,1,0:T(8,128)(2,1)}, bf16[3,192,512]{2,1,0:T(8,128)(2,1)S(1)}, u32[]{:S(2)}) copy-start(bf16[3,192,512]{2,1,0:T(8,128)(2,1)S(1)} %collective-permute-done.7.refs_6_.refs_10_) | copy-start | bytes 1769476
  41.9 35.1 %collective-permute-start.1 = (bf16[3,192,512]{2,1,0:T(8,128)(2,1)S(1)}, bf16[3,192,512]{2,1,0:T(8,128)(2,1)S(1)}, u32[]{:S(2)}, u32[]{:S(2)}) collective-permute-start(bf16[3,192,512]{2,1,0:T(8,128)(2,1)S(1)} %get-tuple-element.47), channel_id=1, source_target_pairs={{0,2},{2,4},{4,6},{6,0},{1,3},{3,5},{5,7},{7,1},{8,10},{10,12},{12... | collective-permute-start | bytes 1769480 | tf_op jit(solution)/shard_map/ppermute | solution.py:147
  54.7 25.2 %copy-start.2 = (bf16[3,192,512]{2,1,0:T(8,128)(2,1)}, bf16[3,192,512]{2,1,0:T(8,128)(2,1)S(1)}, u32[]{:S(2)}) copy-start(bf16[3,192,512]{2,1,0:T(8,128)(2,1)S(1)} %collective-permute-done.9.refs_7_.refs_11_) | copy-start | bytes 1769476
  54.7 25.2 %collective-permute-start.2 = (bf16[3,192,512]{2,1,0:T(8,128)(2,1)S(1)}, bf16[3,192,512]{2,1,0:T(8,128)(2,1)S(1)}, u32[]{:S(2)}, u32[]{:S(2)}) collective-permute-start(bf16[3,192,512]{2,1,0:T(8,128)(2,1)S(1)} %get-tuple-element.48), channel_id=1, source_target_pairs={{0,4},{2,6},{4,0},{6,2},{1,5},{3,7},{5,1},{7,3},{8,12},{10,14},{12... | collective-permute-start | bytes 1769480 | tf_op jit(solution)/shard_map/ppermute | solution.py:147
  58.3 21.5 %copy-start.4 = (bf16[3,192,512]{2,1,0:T(8,128)(2,1)}, bf16[3,192,512]{2,1,0:T(8,128)(2,1)S(1)}, u32[]{:S(2)}) copy-start(bf16[3,192,512]{2,1,0:T(8,128)(2,1)S(1)} %collective-permute-done.5.refs_5_.refs_9_) | copy-start | bytes 1769476
  58.3 5.8 %collective-permute-start.8 = (bf16[192,512]{1,0:T(8,128)(2,1)S(1)}, bf16[192,512]{1,0:T(8,128)(2,1)S(1)}, u32[]{:S(2)}, u32[]{:S(2)}) collective-permute-start(bf16[192,512]{1,0:T(8,128)(2,1)S(1)} %slice_bitcast_fusion.1), channel_id=1, source_target_pairs={{0,1},{1,0},{2,3},{3,2},{4,5},{5,4},{6,7},{7,6},{8,9},{9,8},{10,11... | collective-permute-start | bytes 589832 | tf_op jit(solution)/shard_map/ppermute | solution.py:144
  62.2 4.4 %collective-permute-start.10 = (bf16[192,512]{1,0:T(8,128)(2,1)S(1)}, bf16[192,512]{1,0:T(8,128)(2,1)S(1)}, u32[]{:S(2)}, u32[]{:S(2)}) collective-permute-start(bf16[192,512]{1,0:T(8,128)(2,1)S(1)} %slice_bitcast_fusion), channel_id=1, source_target_pairs={{0,1},{1,0},{2,3},{3,2},{4,5},{5,4},{6,7},{7,6},{8,9},{9,8},{10,11... | collective-permute-start | bytes 589832 | tf_op jit(solution)/shard_map/ppermute | solution.py:144
  64.1 3.5 %collective-permute-start.6 = (bf16[192,512]{1,0:T(8,128)(2,1)S(1)}, bf16[192,512]{1,0:T(8,128)(2,1)S(1)}, u32[]{:S(2)}, u32[]{:S(2)}) collective-permute-start(bf16[192,512]{1,0:T(8,128)(2,1)S(1)} %slice_bitcast_fusion.2), channel_id=1, source_target_pairs={{0,1},{1,0},{2,3},{3,2},{4,5},{5,4},{6,7},{7,6},{8,9},{9,8},{10,11... | collective-permute-start | bytes 589832 | tf_op jit(solution)/shard_map/ppermute | solution.py:144
  72.3 46.8 %collective-permute-start.17 = (bf16[512,512]{1,0:T(8,128)(2,1)}, bf16[512,512]{1,0:T(8,128)(2,1)}, u32[]{:S(2)}, u32[]{:S(2)}) collective-permute-start(bf16[512,512]{1,0:T(8,128)(2,1)} %shard_map.68), channel_id=1, source_target_pairs={{0,8},{8,0},{1,9},{9,1},{2,10},{10,2},{3,11},{11,3},{4,12},{12,4},... | collective-permute-start | bytes 1572872 | tf_op jit(solution)/shard_map/ppermute | solution.py:173
  85.5 33.6 %collective-permute-start.16 = (bf16[256,1024]{1,0:T(8,128)(2,1)}, bf16[256,1024]{1,0:T(8,128)(2,1)}, u32[]{:S(2)}, u32[]{:S(2)}) collective-permute-start(bf16[256,1024]{1,0:T(8,128)(2,1)} %constant_dynamic-slice_fusion), channel_id=1, source_target_pairs={{0,1},{1,0},{2,3},{3,2},{4,5},{5,4},{6,7},{7,6},{8,9},{9,8},{10,11... | collective-permute-start | bytes 1572872 | tf_op jit(solution)/shard_map/ppermute | solution.py:144
  89.2 7.0 %collective-permute-start.14 = (bf16[192,512]{1,0:T(8,128)(2,1)S(1)}, bf16[192,512]{1,0:T(8,128)(2,1)S(1)}, u32[]{:S(2)}, u32[]{:S(2)}) collective-permute-start(bf16[192,512]{1,0:T(8,128)(2,1)S(1)} %slice_bitcast_fusion.7), channel_id=1, source_target_pairs={{0,1},{1,0},{2,3},{3,2},{4,5},{5,4},{6,7},{7,6},{8,9},{9,8},{10,11... | collective-permute-start | bytes 589832 | tf_op jit(solution)/shard_map/ppermute | solution.py:144
  91.1 7.5 %collective-permute-start.13 = (bf16[192,512]{1,0:T(8,128)(2,1)S(1)}, bf16[192,512]{1,0:T(8,128)(2,1)S(1)}, u32[]{:S(2)}, u32[]{:S(2)}) collective-permute-start(bf16[192,512]{1,0:T(8,128)(2,1)S(1)} %slice_bitcast_fusion.8), channel_id=1, source_target_pairs={{0,1},{1,0},{2,3},{3,2},{4,5},{5,4},{6,7},{7,6},{8,9},{9,8},{10,11... | collective-permute-start | bytes 589832 | tf_op jit(solution)/shard_map/ppermute | solution.py:144
  93.5 10.5 %collective-permute-start.12 = (bf16[192,512]{1,0:T(8,128)(2,1)}, bf16[192,512]{1,0:T(8,128)(2,1)}, u32[]{:S(2)}, u32[]{:S(2)}) collective-permute-start(bf16[192,512]{1,0:T(8,128)(2,1)} %slice_bitcast_fusion.9), channel_id=1, source_target_pairs={{0,1},{1,0},{2,3},{3,2},{4,5},{5,4},{6,7},{7,6},{8,9},{9,8},{10,11... | collective-permute-start | bytes 589832 | tf_op jit(solution)/shard_map/ppermute | solution.py:144
  96.2 7.9 %collective-permute-start.11 = (bf16[192,512]{1,0:T(8,128)(2,1)}, bf16[192,512]{1,0:T(8,128)(2,1)}, u32[]{:S(2)}, u32[]{:S(2)}) collective-permute-start(bf16[192,512]{1,0:T(8,128)(2,1)} %slice_bitcast_fusion.10), channel_id=1, source_target_pairs={{0,1},{1,0},{2,3},{3,2},{4,5},{5,4},{6,7},{7,6},{8,9},{9,8},{10,11... | collective-permute-start | bytes 589832 | tf_op jit(solution)/shard_map/ppermute | solution.py:144
  99.3 27.2 %collective-permute-start.15 = (bf16[512,512]{1,0:T(8,128)(2,1)}, bf16[512,512]{1,0:T(8,128)(2,1)}, u32[]{:S(2)}, u32[]{:S(2)}) collective-permute-start(bf16[512,512]{1,0:T(8,128)(2,1)} %shard_map.69), channel_id=1, source_target_pairs={{0,8},{8,0},{1,9},{9,1},{2,10},{10,2},{3,11},{11,3},{4,12},{12,4},... | collective-permute-start | bytes 1572872 | tf_op jit(solution)/shard_map/ppermute | solution.py:173
  131.0 43.4 %copy-start.18 = (f32[1,8,2048]{2,1,0:T(8,128)S(1)}, f32[1,8,2048]{2,1,0:T(8,128)}, u32[]{:S(2)}) copy-start(f32[1,8,2048]{2,1,0:T(8,128)} %param.8) | copy-start | bytes 196612
  131.0 43.4 %copy-start.19 = (f32[1,8,2048]{2,1,0:T(8,128)S(1)}, f32[1,8,2048]{2,1,0:T(8,128)}, u32[]{:S(2)}) copy-start(f32[1,8,2048]{2,1,0:T(8,128)} %param.9) | copy-start | bytes 196612
  (18 other events, 75.7 us)

commit v3 on v2

--- a/solution.py
+++ b/solution.py
@@ -20,6 +20,7 @@
 HALF = W2 // 2
 CHUNK = HALF // 2
 BLOCKS = CHUNK // 128
+WIDE = 2
 ROWS = 512
 INV = 1.0 / math.sqrt(TOK * 16)
 
@@ -73,7 +74,7 @@
         for col in (j, j + 1):
             lanes = slice(col * 128, (col + 1) * 128)
             gradient = own_ref[:, lanes] + part_ref[:, lanes].astype(jnp.float32)
-            base = base_ref[0, :, 0, :, lanes].reshape(rows, 128)
+            base = base_ref[:, :, 0, :, lanes].reshape(rows, 128)
             pseudo = base - (local_ref[:, lanes].astype(jnp.float32) - gradient)
             scale = (jnp.max(jnp.abs(pseudo), axis=1, keepdims=True) + EPSILON).astype(jnp.bfloat16).astype(jnp.float32)
             level = pseudo * (7.0 / scale)
@@ -84,17 +85,18 @@
             for coef in SINE[-2::-1]:
                 poly = poly * square + coef
             code = (step + off * square * poly).astype(jnp.bfloat16).astype(jnp.float32)
-            restored.append((code * (scale * (1.0 / 7.0))).reshape(Z, 8, 128))
-        block = jnp.concatenate(restored, axis=1).astype(jnp.bfloat16)
-        out_ref[0, :, 0, j * 8:(j + 2) * 8, :] = block
+            restored.append((code * (scale * (1.0 / 7.0))).reshape(WIDE, Z, 8, 128))
+        block = jnp.concatenate(restored, axis=2).astype(jnp.bfloat16)
+        out_ref[:, :, 0, j * 8:(j + 2) * 8, :] = block
 
 
 def quantize(own, part, local, base, chunk, earlier=None):
-    rows = 8 * Z
-    tile = pl.BlockSpec((rows, CHUNK), lambda c, i: (c * YLO + i, 0))
-    local_tile = pl.BlockSpec((rows, CHUNK), lambda c, i: (c * YLO + i, chunk))
-    out_tile = pl.BlockSpec((1, Z, 1, BLOCKS * 8, 128), lambda c, i: (i, 0, c, chunk, 0))
-    base_tile = pl.BlockSpec((1, Z, 1, 8, CHUNK), lambda c, i: (i, 0, c, 0, chunk))
+    steps = YLO // WIDE
+    rows = WIDE * 8 * Z
+    tile = pl.BlockSpec((rows, CHUNK), lambda c, i: (c * steps + i, 0))
+    local_tile = pl.BlockSpec((rows, CHUNK), lambda c, i: (c * steps + i, chunk))
+    out_tile = pl.BlockSpec((WIDE, Z, 1, BLOCKS * 8, 128), lambda c, i: (i, 0, c, chunk, 0))
+    base_tile = pl.BlockSpec((WIDE, Z, 1, 8, CHUNK), lambda c, i: (i, 0, c, 0, chunk))
     operands, specs, kernel, aliases = [own, part, local, base], [tile, tile, local_tile, base_tile], quantize_kernel, {}
     if earlier is not None:
         operands.append(earlier)
@@ -102,12 +104,12 @@
         kernel, aliases = (lambda *refs: quantize_kernel(*refs[:4], refs[5])), {4: 0}
     return pl.pallas_call(
         kernel,
-        grid=(2, YLO),
+        grid=(2, steps),
         out_shape=jax.ShapeDtypeStruct((YLO, Z, 2, 2 * BLOCKS * 8, 128), jnp.bfloat16),
         in_specs=specs,
         out_specs=out_tile,
         input_output_aliases=aliases,
-        compiler_params=pltpu.CompilerParams(vmem_limit_bytes=5 * 1024 * 1024),
+        compiler_params=pltpu.CompilerParams(vmem_limit_bytes=6 * 1024 * 1024),
         cost_estimate=COST,
     )(*operands)
 

time: 177 us -> 175 us (0.989)
  Pallas kernels: 26.2 us -> 22.9 us
    pallas_call x2, Pallas kernels: 9.23 us -> 5.92 us  [quantize(): pl.pallas_call(kernel, grid=(2, steps), out_shape=jax.ShapeDtypeStruct((Y...]
  transfers between devices with their start and end apart: 19 -> 19, of which waited for: 4 -> 4; matrix products, arithmetic and copies ran while one was open for 4% -> 4% of each run, Pallas kernels for 12% -> 11%
where the time goes in v3:
time: 175 us; the launch traced here: 174 us
  starting transfers between devices  70.4 us (40%)
  blocking collectives  45 us (26%)
  Pallas kernels  22.9 us (13%)
  local copies, waits for them, and re-layouts  17.5 us (10%)
  waiting for transfers between devices  14.7 us (8%)
  other arithmetic  1.78 us (1%)
    all_to_all x1, blocking collectives, all_to_all(): return lax.all_to_all(array, axes, 0, 0, tiled=True)  45 us
    ppermute x10, starting transfers between devices, other_core(): return lax.ppermute(array, 'c', shift(2, 1))  24.7 us
    ppermute x6, starting transfers between devices, along_x(): return lax.ppermute(array, 'x', shift(X, k))  20.6 us
    pallas_call x4, Pallas kernels, matmul(): pl.pallas_call(matmul_kernel, out_shape=jax.ShapeDtypeStruct((ROWS, CHUNK...  16.1 us
    all_to_all x1, starting transfers between devices, all_to_all(): return lax.all_to_all(array, axes, 0, 0, tiled=True)  15.5 us
    ppermute x6, waiting for transfers between devices, along_x(): return lax.ppermute(array, 'x', shift(X, k))  13.7 us
    unnamed x46, local copies, waits for them, and re-layouts  10.2 us
    ppermute x2, starting transfers between devices, body(): far = [lax.ppermute(part, 'yhi', shift(2, 1)) for part in sent_far]  9.49 us
  transfers between devices with their start and end apart: 19, of which 4 were waited for; matrix products, arithmetic and copies ran while one was open for 4% of the time, Pallas kernels for 11%

profile of v3, /device:TPU:1, one launch (start us, length us, event | category | flops | bytes accessed | tf_op | source)
XLA Modules:
  0.0 173.6 jit_solution(8962460462725859178)
XLA Ops:
  0.6 2.4 %broadcast_in_dim.12 = f32[32,2,8,1024]{3,2,1,0:T(8,128)} broadcast(f32[2,8,1024]{2,1,0:T(8,128)} %bitcast.43), dimensions={1,2,3} | broadcast | bytes 2162688 | tf_op jit(solution)/shard_map/broadcast_in_dim | solution.py:185
  3.1 15.5 %all-to-all-start = ((f32[64,8,1024]{2,1,0:T(8,128)}), f32[64,8,1024]{2,1,0:T(8,128)S(1)}, u32[]{:S(2)}, u32[]{:S(2)}) async-start(f32[64,8,1024]{2,1,0:T(8,128)} %bitcast.46), calls=%async_computation | async-start | bytes 4194304 | tf_op jit(solution)/shard_map/all_to_all | solution.py:152
  23.8 4.7 %collective-permute-start.7 = (bf16[3,192,512]{2,1,0:T(8,128)(2,1)S(1)}, bf16[3,192,512]{2,1,0:T(8,128)(2,1)S(1)}, u32[]{:S(2)}, u32[]{:S(2)}) collective-permute-start(bf16[3,192,512]{2,1,0:T(8,128)(2,1)S(1)} %get-tuple-element.39), channel_id=1, source_target_pairs={{0,4},{2,6},{4,0},{6,2},{1,5},{3,7},{5,1},{7,3},{8,12},{10,14},{12... | collective-permute-start | bytes 1769480 | tf_op jit(solution)/shard_map/ppermute | solution.py:149
  28.4 2.8 %collective-permute-start.9 = (bf16[3,192,512]{2,1,0:T(8,128)(2,1)S(1)}, bf16[3,192,512]{2,1,0:T(8,128)(2,1)S(1)}, u32[]{:S(2)}, u32[]{:S(2)}) collective-permute-start(bf16[3,192,512]{2,1,0:T(8,128)(2,1)S(1)} %get-tuple-element.40), channel_id=1, source_target_pairs={{0,6},{2,0},{4,2},{6,4},{1,7},{3,1},{5,3},{7,5},{8,14},{10,8},{12,... | collective-permute-start | bytes 1769480 | tf_op jit(solution)/shard_map/ppermute | solution.py:149
  31.2 2.7 %collective-permute-start.4 = (bf16[192,512]{1,0:T(8,128)(2,1)S(1)}, bf16[192,512]{1,0:T(8,128)(2,1)S(1)}, u32[]{:S(2)}, u32[]{:S(2)}) collective-permute-start(bf16[192,512]{1,0:T(8,128)(2,1)S(1)} %bitcast.49), channel_id=1, source_target_pairs={{0,1},{1,0},{2,3},{3,2},{4,5},{5,4},{6,7},{7,6},{8,9},{9,8},{10,11... | collective-permute-start | bytes 589832 | tf_op jit(solution)/shard_map/ppermute | solution.py:146
  33.9 2.5 %collective-permute-start.5 = (bf16[3,192,512]{2,1,0:T(8,128)(2,1)S(1)}, bf16[3,192,512]{2,1,0:T(8,128)(2,1)S(1)}, u32[]{:S(2)}, u32[]{:S(2)}) collective-permute-start(bf16[3,192,512]{2,1,0:T(8,128)(2,1)S(1)} %get-tuple-element.41), channel_id=1, source_target_pairs={{0,2},{2,4},{4,6},{6,0},{1,3},{3,5},{5,7},{7,1},{8,10},{10,12},{12... | collective-permute-start | bytes 1769480 | tf_op jit(solution)/shard_map/ppermute | solution.py:149
  36.6 4.0 %collective-permute-start.3 = (bf16[3,192,512]{2,1,0:T(8,128)(2,1)S(1)}, bf16[3,192,512]{2,1,0:T(8,128)(2,1)S(1)}, u32[]{:S(2)}, u32[]{:S(2)}) collective-permute-start(bf16[3,192,512]{2,1,0:T(8,128)(2,1)S(1)} %get-tuple-element.46), channel_id=1, source_target_pairs={{0,6},{2,0},{4,2},{6,4},{1,7},{3,1},{5,3},{7,5},{8,14},{10,8},{12,... | collective-permute-start | bytes 1769480 | tf_op jit(solution)/shard_map/ppermute | solution.py:149
  41.9 3.1 %collective-permute-start.1 = (bf16[3,192,512]{2,1,0:T(8,128)(2,1)S(1)}, bf16[3,192,512]{2,1,0:T(8,128)(2,1)S(1)}, u32[]{:S(2)}, u32[]{:S(2)}) collective-permute-start(bf16[3,192,512]{2,1,0:T(8,128)(2,1)S(1)} %get-tuple-element.47), channel_id=1, source_target_pairs={{0,2},{2,4},{4,6},{6,0},{1,3},{3,5},{5,7},{7,1},{8,10},{10,12},{12... | collective-permute-start | bytes 1769480 | tf_op jit(solution)/shard_map/ppermute | solution.py:149
  45.1 9.6 %collective-permute-done.9.refs_7_.refs_11_ = bf16[3,192,512]{2,1,0:T(8,128)(2,1)S(1)} collective-permute-done((bf16[3,192,512]{2,1,0:T(8,128)(2,1)S(1)}, bf16[3,192,512]{2,1,0:T(8,128)(2,1)S(1)}, u32[]{:S(2)}, u32[]{:S(2)}) %collective-permute-start.9) | collective-permute-done | bytes 589856 | tf_op jit(solution)/shard_map/ppermute | solution.py:149
  54.7 3.6 %collective-permute-start.2 = (bf16[3,192,512]{2,1,0:T(8,128)(2,1)S(1)}, bf16[3,192,512]{2,1,0:T(8,128)(2,1)S(1)}, u32[]{:S(2)}, u32[]{:S(2)}) collective-permute-start(bf16[3,192,512]{2,1,0:T(8,128)(2,1)S(1)} %get-tuple-element.48), channel_id=1, source_target_pairs={{0,4},{2,6},{4,0},{6,2},{1,5},{3,7},{5,1},{7,3},{8,12},{10,14},{12... | collective-permute-start | bytes 1769480 | tf_op jit(solution)/shard_map/ppermute | solution.py:149
  58.3 3.8 %collective-permute-start.8 = (bf16[192,512]{1,0:T(8,128)(2,1)S(1)}, bf16[192,512]{1,0:T(8,128)(2,1)S(1)}, u32[]{:S(2)}, u32[]{:S(2)}) collective-permute-start(bf16[192,512]{1,0:T(8,128)(2,1)S(1)} %slice_bitcast_fusion.1), channel_id=1, source_target_pairs={{0,1},{1,0},{2,3},{3,2},{4,5},{5,4},{6,7},{7,6},{8,9},{9,8},{10,11... | collective-permute-start | bytes 589832 | tf_op jit(solution)/shard_map/ppermute | solution.py:146
  64.1 2.4 %collective-permute-start.6 = (bf16[192,512]{1,0:T(8,128)(2,1)S(1)}, bf16[192,512]{1,0:T(8,128)(2,1)S(1)}, u32[]{:S(2)}, u32[]{:S(2)}) collective-permute-start(bf16[192,512]{1,0:T(8,128)(2,1)S(1)} %slice_bitcast_fusion.2), channel_id=1, source_target_pairs={{0,1},{1,0},{2,3},{3,2},{4,5},{5,4},{6,7},{7,6},{8,9},{9,8},{10,11... | collective-permute-start | bytes 589832 | tf_op jit(solution)/shard_map/ppermute | solution.py:146
  67.6 4.7 %shard_map.68 = bf16[512,512]{1,0:T(8,128)(2,1)} custom-call(bf16[192,512]{1,0:T(8,128)(2,1)S(1)} %collective-permute-done.4.refs_0_, bf16[192,512]{1,0:T(8,128)(2,1)S(1)} %collective-permute-done.6.refs_1_, bf16[192,512]{1,0:T(8,128)(2,1)S(1)} %collective-permute-done.8.refs_2_, bf16[192,512]{1,0:T(8,128)(2,1)S(1)} %collective-permute-done.10.refs_3_, ...), custom_call_target="tpu_custom_call" | custom-call | flops 1 | bytes 1 | tf_op jit(solution)/shard_map/pallas_call | solution.py:55
  72.3 4.8 %collective-permute-start.17 = (bf16[512,512]{1,0:T(8,128)(2,1)}, bf16[512,512]{1,0:T(8,128)(2,1)}, u32[]{:S(2)}, u32[]{:S(2)}) collective-permute-start(bf16[512,512]{1,0:T(8,128)(2,1)} %shard_map.68), channel_id=1, source_target_pairs={{0,8},{8,0},{1,9},{9,1},{2,10},{10,2},{3,11},{11,3},{4,12},{12,4},... | collective-permute-start | bytes 1572872 | tf_op jit(solution)/shard_map/ppermute | solution.py:175
  77.1 2.8 %collective-permute-done.2.refs_10_.refs_6_ = bf16[3,192,512]{2,1,0:T(8,128)(2,1)S(1)} collective-permute-done((bf16[3,192,512]{2,1,0:T(8,128)(2,1)S(1)}, bf16[3,192,512]{2,1,0:T(8,128)(2,1)S(1)}, u32[]{:S(2)}, u32[]{:S(2)}) %collective-permute-start.2) | collective-permute-done | bytes 589856 | tf_op jit(solution)/shard_map/ppermute | solution.py:149
  79.9 4.7 %shard_map.69 = bf16[512,512]{1,0:T(8,128)(2,1)} custom-call(bf16[192,512]{1,0:T(8,128)(2,1)S(1)} %collective-permute-done.4.refs_0_, bf16[192,512]{1,0:T(8,128)(2,1)S(1)} %collective-permute-done.6.refs_1_, bf16[192,512]{1,0:T(8,128)(2,1)S(1)} %collective-permute-done.8.refs_2_, bf16[192,512]{1,0:T(8,128)(2,1)S(1)} %collective-permute-done.10.refs_3_, ...), custom_call_target="tpu_custom_call" | custom-call | flops 1 | bytes 1 | tf_op jit(solution)/shard_map/pallas_call | solution.py:55
  85.5 2.9 %collective-permute-start.16 = (bf16[256,1024]{1,0:T(8,128)(2,1)}, bf16[256,1024]{1,0:T(8,128)(2,1)}, u32[]{:S(2)}, u32[]{:S(2)}) collective-permute-start(bf16[256,1024]{1,0:T(8,128)(2,1)} %constant_dynamic-slice_fusion), channel_id=1, source_target_pairs={{0,1},{1,0},{2,3},{3,2},{4,5},{5,4},{6,7},{7,6},{8,9},{9,8},{10,11... | collective-permute-start | bytes 1572872 | tf_op jit(solution)/shard_map/ppermute | solution.py:146
  91.1 2.4 %collective-permute-start.13 = (bf16[192,512]{1,0:T(8,128)(2,1)S(1)}, bf16[192,512]{1,0:T(8,128)(2,1)S(1)}, u32[]{:S(2)}, u32[]{:S(2)}) collective-permute-start(bf16[192,512]{1,0:T(8,128)(2,1)S(1)} %slice_bitcast_fusion.8), channel_id=1, source_target_pairs={{0,1},{1,0},{2,3},{3,2},{4,5},{5,4},{6,7},{7,6},{8,9},{9,8},{10,11... | collective-permute-start | bytes 589832 | tf_op jit(solution)/shard_map/ppermute | solution.py:146
  99.3 4.7 %collective-permute-start.15 = (bf16[512,512]{1,0:T(8,128)(2,1)}, bf16[512,512]{1,0:T(8,128)(2,1)}, u32[]{:S(2)}, u32[]{:S(2)}) collective-permute-start(bf16[512,512]{1,0:T(8,128)(2,1)} %shard_map.69), channel_id=1, source_target_pairs={{0,8},{8,0},{1,9},{9,1},{2,10},{10,2},{3,11},{11,3},{4,12},{12,4},... | collective-permute-start | bytes 1572872 | tf_op jit(solution)/shard_map/ppermute | solution.py:175
  111.3 3.4 %shard_map.71.own_ref = f32[512,512]{1,0:T(8,128)S(1)} custom-call(bf16[192,512]{1,0:T(8,128)(2,1)} %collective-permute-done.11.refs_0_, bf16[192,512]{1,0:T(8,128)(2,1)} %collective-permute-done.12.refs_1_, bf16[192,512]{1,0:T(8,128)(2,1)S(1)} %copy-done.17, bf16[192,512]{1,0:T(8,128)(2,1)S(1)} %collective-permute-done.14.refs_3_, ...), custom_call_target="tpu_custom_call" | custom-call | flops 1 | bytes 1 | tf_op jit(solution)/shard_map/pallas_call | solution.py:55
  114.7 3.4 %shard_map.70.refs_0_ = f32[512,512]{1,0:T(8,128)S(1)} custom-call(bf16[192,512]{1,0:T(8,128)(2,1)} %collective-permute-done.11.refs_0_, bf16[192,512]{1,0:T(8,128)(2,1)} %collective-permute-done.12.refs_1_, bf16[192,512]{1,0:T(8,128)(2,1)S(1)} %copy-done.17, bf16[192,512]{1,0:T(8,128)(2,1)S(1)} %collective-permute-done.14.refs_3_, ...), custom_call_target="tpu_custom_call" | custom-call | flops 1 | bytes 1 | tf_op jit(solution)/shard_map/pallas_call | solution.py:55
  121.7 3.0 %shard_map.72.refs_4_ = bf16[4,8,2,64,128]{4,3,2,1,0:T(8,128)(2,1)S(1)} custom-call(f32[512,512]{1,0:T(8,128)S(1)} %copy-done.15, bf16[512,512]{1,0:T(8,128)(2,1)} %collective-permute-done.17.part_ref, bf16[512,1024]{1,0:T(8,128)(2,1)S(1)} %pad_maximum_fusion.local_ref.refs_2_, f32[4,8,2,8,1024]{4,3,2,1,0:T(8,128)S(1)} %bitcast.39), custom_call_target="tpu_custom_call" | custom-call | flops 1 | bytes 1 | tf_op jit(solution)/shard_map/pallas_call | solution.py:105
  124.8 2.9 %shard_map.73 = bf16[4,8,2,64,128]{4,3,2,1,0:T(8,128)(2,1)S(1)} custom-call(f32[512,512]{1,0:T(8,128)S(1)} %copy-done.13, bf16[512,512]{1,0:T(8,128)(2,1)} %collective-permute-done.15.refs_1_, bf16[512,1024]{1,0:T(8,128)(2,1)S(1)} %pad_maximum_fusion.local_ref.refs_2_, f32[4,8,2,8,1024]{4,3,2,1,0:T(8,128)S(1)} %bitcast.40, ...), custom_call_target="tpu_custom_call", output_to_operand_aliasing={{}: (4, {})} | custom-call | flops 1 | bytes 1 | tf_op jit(solution)/shard_map/pallas_call | solution.py:105
  127.7 45.0 %all_to_all.10 = bf16[64,64,128]{2,1,0:T(8,128)(2,1)S(1)} all-to-all(bf16[64,64,128]{2,1,0:T(8,128)(2,1)S(1)} %bitcast.41), channel_id=1, replica_groups=mesh['ylo'=4,'z'=8,'yhi'=2,'x'=4,'c'=2] {'ylo','z','c'}, dimensions={0} | all-to-all | bytes 2097152 | tf_op jit(solution)/shard_map/all_to_all | solution.py:152
  (85 shorter events, 30.5 us)
Async XLA Ops:
  3.1 117.4 %all-to-all-start = ((f32[64,8,1024]{2,1,0:T(8,128)}), f32[64,8,1024]{2,1,0:T(8,128)S(1)}, u32[]{:S(2)}, u32[]{:S(2)}) async-start(f32[64,8,1024]{2,1,0:T(8,128)} %bitcast.46), calls=%async_computation | async-start | bytes 4194304 | tf_op jit(solution)/shard_map/all_to_all | solution.py:152
  19.5 4.0 %collective-permute-start = (bf16[192,1024]{1,0:T(8,128)(2,1)}, bf16[192,1024]{1,0:T(8,128)(2,1)S(1)}, u32[]{:S(2)}, u32[]{:S(2)}) collective-permute-start(bf16[192,1024]{1,0:T(8,128)(2,1)} %get-tuple-element.37), channel_id=1, source_target_pairs={{0,1},{1,0},{2,3},{3,2},{4,5},{5,4},{6,7},{7,6},{8,9},{9,8},{10,11... | collective-permute-start | bytes 1179656 | tf_op jit(solution)/shard_map/ppermute | solution.py:146
  23.8 18.2 %collective-permute-start.7 = (bf16[3,192,512]{2,1,0:T(8,128)(2,1)S(1)}, bf16[3,192,512]{2,1,0:T(8,128)(2,1)S(1)}, u32[]{:S(2)}, u32[]{:S(2)}) collective-permute-start(bf16[3,192,512]{2,1,0:T(8,128)(2,1)S(1)} %get-tuple-element.39), channel_id=1, source_target_pairs={{0,4},{2,6},{4,0},{6,2},{1,5},{3,7},{5,1},{7,3},{8,12},{10,14},{12... | collective-permute-start | bytes 1769480 | tf_op jit(solution)/shard_map/ppermute | solution.py:149
  28.4 26.2 %collective-permute-start.9 = (bf16[3,192,512]{2,1,0:T(8,128)(2,1)S(1)}, bf16[3,192,512]{2,1,0:T(8,128)(2,1)S(1)}, u32[]{:S(2)}, u32[]{:S(2)}) collective-permute-start(bf16[3,192,512]{2,1,0:T(8,128)(2,1)S(1)} %get-tuple-element.40), channel_id=1, source_target_pairs={{0,6},{2,0},{4,2},{6,4},{1,7},{3,1},{5,3},{7,5},{8,14},{10,8},{12,... | collective-permute-start | bytes 1769480 | tf_op jit(solution)/shard_map/ppermute | solution.py:149
  31.2 31.0 %collective-permute-start.4 = (bf16[192,512]{1,0:T(8,128)(2,1)S(1)}, bf16[192,512]{1,0:T(8,128)(2,1)S(1)}, u32[]{:S(2)}, u32[]{:S(2)}) collective-permute-start(bf16[192,512]{1,0:T(8,128)(2,1)S(1)} %bitcast.49), channel_id=1, source_target_pairs={{0,1},{1,0},{2,3},{3,2},{4,5},{5,4},{6,7},{7,6},{8,9},{9,8},{10,11... | collective-permute-start | bytes 589832 | tf_op jit(solution)/shard_map/ppermute | solution.py:146
  33.9 24.4 %collective-permute-start.5 = (bf16[3,192,512]{2,1,0:T(8,128)(2,1)S(1)}, bf16[3,192,512]{2,1,0:T(8,128)(2,1)S(1)}, u32[]{:S(2)}, u32[]{:S(2)}) collective-permute-start(bf16[3,192,512]{2,1,0:T(8,128)(2,1)S(1)} %get-tuple-element.41), channel_id=1, source_target_pairs={{0,2},{2,4},{4,6},{6,0},{1,3},{3,5},{5,7},{7,1},{8,10},{10,12},{12... | collective-permute-start | bytes 1769480 | tf_op jit(solution)/shard_map/ppermute | solution.py:149
  36.6 40.4 %collective-permute-start.3 = (bf16[3,192,512]{2,1,0:T(8,128)(2,1)S(1)}, bf16[3,192,512]{2,1,0:T(8,128)(2,1)S(1)}, u32[]{:S(2)}, u32[]{:S(2)}) collective-permute-start(bf16[3,192,512]{2,1,0:T(8,128)(2,1)S(1)} %get-tuple-element.46), channel_id=1, source_target_pairs={{0,6},{2,0},{4,2},{6,4},{1,7},{3,1},{5,3},{7,5},{8,14},{10,8},{12,... | collective-permute-start | bytes 1769480 | tf_op jit(solution)/shard_map/ppermute | solution.py:149
  41.9 37.9 %copy-start = (bf16[3,192,512]{2,1,0:T(8,128)(2,1)}, bf16[3,192,512]{2,1,0:T(8,128)(2,1)S(1)}, u32[]{:S(2)}) copy-start(bf16[3,192,512]{2,1,0:T(8,128)(2,1)S(1)} %collective-permute-done.7.refs_6_.refs_10_) | copy-start | bytes 1769476
  41.9 35.1 %collective-permute-start.1 = (bf16[3,192,512]{2,1,0:T(8,128)(2,1)S(1)}, bf16[3,192,512]{2,1,0:T(8,128)(2,1)S(1)}, u32[]{:S(2)}, u32[]{:S(2)}) collective-permute-start(bf16[3,192,512]{2,1,0:T(8,128)(2,1)S(1)} %get-tuple-element.47), channel_id=1, source_target_pairs={{0,2},{2,4},{4,6},{6,0},{1,3},{3,5},{5,7},{7,1},{8,10},{10,12},{12... | collective-permute-start | bytes 1769480 | tf_op jit(solution)/shard_map/ppermute | solution.py:149
  54.7 25.2 %copy-start.2 = (bf16[3,192,512]{2,1,0:T(8,128)(2,1)}, bf16[3,192,512]{2,1,0:T(8,128)(2,1)S(1)}, u32[]{:S(2)}) copy-start(bf16[3,192,512]{2,1,0:T(8,128)(2,1)S(1)} %collective-permute-done.9.refs_7_.refs_11_) | copy-start | bytes 1769476
  54.7 25.2 %collective-permute-start.2 = (bf16[3,192,512]{2,1,0:T(8,128)(2,1)S(1)}, bf16[3,192,512]{2,1,0:T(8,128)(2,1)S(1)}, u32[]{:S(2)}, u32[]{:S(2)}) collective-permute-start(bf16[3,192,512]{2,1,0:T(8,128)(2,1)S(1)} %get-tuple-element.48), channel_id=1, source_target_pairs={{0,4},{2,6},{4,0},{6,2},{1,5},{3,7},{5,1},{7,3},{8,12},{10,14},{12... | collective-permute-start | bytes 1769480 | tf_op jit(solution)/shard_map/ppermute | solution.py:149
  58.3 21.5 %copy-start.4 = (bf16[3,192,512]{2,1,0:T(8,128)(2,1)}, bf16[3,192,512]{2,1,0:T(8,128)(2,1)S(1)}, u32[]{:S(2)}) copy-start(bf16[3,192,512]{2,1,0:T(8,128)(2,1)S(1)} %collective-permute-done.5.refs_5_.refs_9_) | copy-start | bytes 1769476
  58.3 5.8 %collective-permute-start.8 = (bf16[192,512]{1,0:T(8,128)(2,1)S(1)}, bf16[192,512]{1,0:T(8,128)(2,1)S(1)}, u32[]{:S(2)}, u32[]{:S(2)}) collective-permute-start(bf16[192,512]{1,0:T(8,128)(2,1)S(1)} %slice_bitcast_fusion.1), channel_id=1, source_target_pairs={{0,1},{1,0},{2,3},{3,2},{4,5},{5,4},{6,7},{7,6},{8,9},{9,8},{10,11... | collective-permute-start | bytes 589832 | tf_op jit(solution)/shard_map/ppermute | solution.py:146
  62.2 4.4 %collective-permute-start.10 = (bf16[192,512]{1,0:T(8,128)(2,1)S(1)}, bf16[192,512]{1,0:T(8,128)(2,1)S(1)}, u32[]{:S(2)}, u32[]{:S(2)}) collective-permute-start(bf16[192,512]{1,0:T(8,128)(2,1)S(1)} %slice_bitcast_fusion), channel_id=1, source_target_pairs={{0,1},{1,0},{2,3},{3,2},{4,5},{5,4},{6,7},{7,6},{8,9},{9,8},{10,11... | collective-permute-start | bytes 589832 | tf_op jit(solution)/shard_map/ppermute | solution.py:146
  64.1 3.5 %collective-permute-start.6 = (bf16[192,512]{1,0:T(8,128)(2,1)S(1)}, bf16[192,512]{1,0:T(8,128)(2,1)S(1)}, u32[]{:S(2)}, u32[]{:S(2)}) collective-permute-start(bf16[192,512]{1,0:T(8,128)(2,1)S(1)} %slice_bitcast_fusion.2), channel_id=1, source_target_pairs={{0,1},{1,0},{2,3},{3,2},{4,5},{5,4},{6,7},{7,6},{8,9},{9,8},{10,11... | collective-permute-start | bytes 589832 | tf_op jit(solution)/shard_map/ppermute | solution.py:146
  72.3 46.8 %collective-permute-start.17 = (bf16[512,512]{1,0:T(8,128)(2,1)}, bf16[512,512]{1,0:T(8,128)(2,1)}, u32[]{:S(2)}, u32[]{:S(2)}) collective-permute-start(bf16[512,512]{1,0:T(8,128)(2,1)} %shard_map.68), channel_id=1, source_target_pairs={{0,8},{8,0},{1,9},{9,1},{2,10},{10,2},{3,11},{11,3},{4,12},{12,4},... | collective-permute-start | bytes 1572872 | tf_op jit(solution)/shard_map/ppermute | solution.py:175
  85.5 33.6 %collective-permute-start.16 = (bf16[256,1024]{1,0:T(8,128)(2,1)}, bf16[256,1024]{1,0:T(8,128)(2,1)}, u32[]{:S(2)}, u32[]{:S(2)}) collective-permute-start(bf16[256,1024]{1,0:T(8,128)(2,1)} %constant_dynamic-slice_fusion), channel_id=1, source_target_pairs={{0,1},{1,0},{2,3},{3,2},{4,5},{5,4},{6,7},{7,6},{8,9},{9,8},{10,11... | collective-permute-start | bytes 1572872 | tf_op jit(solution)/shard_map/ppermute | solution.py:146
  89.2 7.0 %collective-permute-start.14 = (bf16[192,512]{1,0:T(8,128)(2,1)S(1)}, bf16[192,512]{1,0:T(8,128)(2,1)S(1)}, u32[]{:S(2)}, u32[]{:S(2)}) collective-permute-start(bf16[192,512]{1,0:T(8,128)(2,1)S(1)} %slice_bitcast_fusion.7), channel_id=1, source_target_pairs={{0,1},{1,0},{2,3},{3,2},{4,5},{5,4},{6,7},{7,6},{8,9},{9,8},{10,11... | collective-permute-start | bytes 589832 | tf_op jit(solution)/shard_map/ppermute | solution.py:146
  91.1 7.5 %collective-permute-start.13 = (bf16[192,512]{1,0:T(8,128)(2,1)S(1)}, bf16[192,512]{1,0:T(8,128)(2,1)S(1)}, u32[]{:S(2)}, u32[]{:S(2)}) collective-permute-start(bf16[192,512]{1,0:T(8,128)(2,1)S(1)} %slice_bitcast_fusion.8), channel_id=1, source_target_pairs={{0,1},{1,0},{2,3},{3,2},{4,5},{5,4},{6,7},{7,6},{8,9},{9,8},{10,11... | collective-permute-start | bytes 589832 | tf_op jit(solution)/shard_map/ppermute | solution.py:146
  93.5 10.5 %collective-permute-start.12 = (bf16[192,512]{1,0:T(8,128)(2,1)}, bf16[192,512]{1,0:T(8,128)(2,1)}, u32[]{:S(2)}, u32[]{:S(2)}) collective-permute-start(bf16[192,512]{1,0:T(8,128)(2,1)} %slice_bitcast_fusion.9), channel_id=1, source_target_pairs={{0,1},{1,0},{2,3},{3,2},{4,5},{5,4},{6,7},{7,6},{8,9},{9,8},{10,11... | collective-permute-start | bytes 589832 | tf_op jit(solution)/shard_map/ppermute | solution.py:146
  96.2 7.9 %collective-permute-start.11 = (bf16[192,512]{1,0:T(8,128)(2,1)}, bf16[192,512]{1,0:T(8,128)(2,1)}, u32[]{:S(2)}, u32[]{:S(2)}) collective-permute-start(bf16[192,512]{1,0:T(8,128)(2,1)} %slice_bitcast_fusion.10), channel_id=1, source_target_pairs={{0,1},{1,0},{2,3},{3,2},{4,5},{5,4},{6,7},{7,6},{8,9},{9,8},{10,11... | collective-permute-start | bytes 589832 | tf_op jit(solution)/shard_map/ppermute | solution.py:146
  99.3 25.5 %collective-permute-start.15 = (bf16[512,512]{1,0:T(8,128)(2,1)}, bf16[512,512]{1,0:T(8,128)(2,1)}, u32[]{:S(2)}, u32[]{:S(2)}) collective-permute-start(bf16[512,512]{1,0:T(8,128)(2,1)} %shard_map.69), channel_id=1, source_target_pairs={{0,8},{8,0},{1,9},{9,1},{2,10},{10,2},{3,11},{11,3},{4,12},{12,4},... | collective-permute-start | bytes 1572872 | tf_op jit(solution)/shard_map/ppermute | solution.py:175
  127.7 45.1 %copy-start.18 = (f32[1,8,2048]{2,1,0:T(8,128)S(1)}, f32[1,8,2048]{2,1,0:T(8,128)}, u32[]{:S(2)}) copy-start(f32[1,8,2048]{2,1,0:T(8,128)} %param.8) | copy-start | bytes 196612
  127.7 45.1 %copy-start.19 = (f32[1,8,2048]{2,1,0:T(8,128)S(1)}, f32[1,8,2048]{2,1,0:T(8,128)}, u32[]{:S(2)}) copy-start(f32[1,8,2048]{2,1,0:T(8,128)} %param.9) | copy-start | bytes 196612
  (18 other events, 74.0 us)

commit v4 on v3

--- a/solution.py
+++ b/solution.py
@@ -31,23 +31,11 @@
 
 def matmul_kernel(*refs):
     others, features, columns, out_ref = refs[:X], refs[X:2 * X], refs[2 * X:3 * X], refs[3 * X]
-    a_all, c_all, sems = refs[3 * X + 1:]
-    copies = []
-    for k in range(X):
-        copies.append((others[k], a_all.at[k, 1]))
-        copies.append((features[k].at[0], a_all.at[k, 0]))
-        copies.append((columns[k].at[1:3], c_all.at[k]))
-    copies = [pltpu.make_async_copy(*ends, sems.at[i]) for i, ends in enumerate(copies)]
-    for copy in copies:
-        copy.start()
-    for copy in copies:
-        copy.wait()
-    everything = c_all[...].reshape(2 * X * TOK, CHUNK)
+    everything = jnp.concatenate([part for ref in columns for part in (ref[1], ref[2])])
     for m in range(2):
         rows = slice(m * 256, (m + 1) * 256)
-        part = lax.dot_general(
-            a_all[:, :, :, rows].reshape(2 * X * TOK, 256), everything, (((0,), (0,)), ((), ())),
-            preferred_element_type=jnp.float32)
+        tokens = jnp.concatenate([part for k in range(X) for part in (features[k][0, :, rows], others[k][:, rows])])
+        part = lax.dot_general(tokens, everything, (((0,), (0,)), ((), ())), preferred_element_type=jnp.float32)
         out_ref[rows, :] = (part * INV).astype(out_ref.dtype)
 
 
@@ -55,14 +43,9 @@
     return pl.pallas_call(
         matmul_kernel,
         out_shape=jax.ShapeDtypeStruct((ROWS, CHUNK), dtype),
-        in_specs=[pl.BlockSpec(memory_space=pl.ANY)] * (3 * X),
+        in_specs=[pl.BlockSpec(memory_space=pltpu.VMEM)] * (3 * X),
         out_specs=pl.BlockSpec(memory_space=pltpu.VMEM),
-        scratch_shapes=[
-            pltpu.VMEM((X, 2, TOK, ROWS), jnp.bfloat16),
-            pltpu.VMEM((X, 2, TOK, CHUNK), jnp.bfloat16),
-            pltpu.SemaphoreType.DMA((3 * X,)),
-        ],
-        compiler_params=pltpu.CompilerParams(vmem_limit_bytes=8 * 1024 * 1024),
+        compiler_params=pltpu.CompilerParams(vmem_limit_bytes=14 * 1024 * 1024),
         cost_estimate=COST,
     )(*others, *features, *columns)
 

time: 175 us -> 172 us (0.983)
  Pallas kernels: 22.9 us -> 14.8 us
  waiting for transfers between devices: 14.7 us -> 17.7 us
  blocking collectives: 45 us -> 47.9 us
    pallas_call x4, Pallas kernels: 16.1 us -> 8.09 us  [matmul(): pl.pallas_call(matmul_kernel, out_shape=jax.ShapeDtypeStruct((ROWS, CHUNK...]
    ppermute x6, waiting for transfers between devices: 13.7 us -> 16.6 us  [along_x(): return lax.ppermute(array, 'x', shift(X, k))]
    all_to_all x1, blocking collectives: 45 us -> 47.9 us  [all_to_all(): return lax.all_to_all(array, axes, 0, 0, tiled=True)]
  transfers between devices with their start and end apart: 19 -> 19, of which waited for: 4 -> 4; matrix products, arithmetic and copies ran while one was open for 4% -> 4% of each run, Pallas kernels for 11% -> 6%
where the time goes in v4:
time: 172 us; the launch traced here: 171 us
  starting transfers between devices  70.3 us (41%)
  blocking collectives  47.9 us (28%)
  waiting for transfers between devices  17.7 us (10%)
  local copies, waits for them, and re-layouts  16.5 us (10%)
  Pallas kernels  14.8 us (9%)
  other arithmetic  2.13 us (1%)
    all_to_all x1, blocking collectives, all_to_all(): return lax.all_to_all(array, axes, 0, 0, tiled=True)  47.9 us
    ppermute x10, starting transfers between devices, other_core(): return lax.ppermute(array, 'c', shift(2, 1))  24.6 us
    ppermute x6, starting transfers between devices, along_x(): return lax.ppermute(array, 'x', shift(X, k))  20.6 us
    ppermute x6, waiting for transfers between devices, along_x(): return lax.ppermute(array, 'x', shift(X, k))  16.6 us
    all_to_all x1, starting transfers between devices, all_to_all(): return lax.all_to_all(array, axes, 0, 0, tiled=True)  15.5 us
    ppermute x2, starting transfers between devices, body(): far = [lax.ppermute(part, 'yhi', shift(2, 1)) for part in sent_far]  9.5 us
    unnamed x46, local copies, waits for them, and re-layouts  9.25 us
    pallas_call x4, Pallas kernels, matmul(): pl.pallas_call(matmul_kernel, out_shape=jax.ShapeDtypeStruct((ROWS, CHUNK...  8.09 us
  transfers between devices with their start and end apart: 19, of which 4 were waited for; matrix products, arithmetic and copies ran while one was open for 4% of the time, Pallas kernels for 6%

profile of v4, /device:TPU:1, one launch (start us, length us, event | category | flops | bytes accessed | tf_op | source)
XLA Modules:
  0.0 170.7 jit_solution(8321619060439632545)
XLA Ops:
  0.6 2.4 %broadcast_in_dim.12 = f32[32,2,8,1024]{3,2,1,0:T(8,128)} broadcast(f32[2,8,1024]{2,1,0:T(8,128)} %bitcast.43), dimensions={1,2,3} | broadcast | bytes 2162688 | tf_op jit(solution)/shard_map/broadcast_in_dim | solution.py:168
  3.1 15.5 %all-to-all-start = ((f32[64,8,1024]{2,1,0:T(8,128)}), f32[64,8,1024]{2,1,0:T(8,128)S(1)}, u32[]{:S(2)}, u32[]{:S(2)}) async-start(f32[64,8,1024]{2,1,0:T(8,128)} %bitcast.46), calls=%async_computation | async-start | bytes 4194304 | tf_op jit(solution)/shard_map/all_to_all | solution.py:135
  19.5 2.4 %collective-permute-start = (bf16[192,1024]{1,0:T(8,128)(2,1)}, bf16[192,1024]{1,0:T(8,128)(2,1)S(1)}, u32[]{:S(2)}, u32[]{:S(2)}) collective-permute-start(bf16[192,1024]{1,0:T(8,128)(2,1)} %get-tuple-element.37), channel_id=1, source_target_pairs={{0,1},{1,0},{2,3},{3,2},{4,5},{5,4},{6,7},{7,6},{8,9},{9,8},{10,11... | collective-permute-start | bytes 1179656 | tf_op jit(solution)/shard_map/ppermute | solution.py:129
  23.8 4.7 %collective-permute-start.7 = (bf16[3,192,512]{2,1,0:T(8,128)(2,1)S(1)}, bf16[3,192,512]{2,1,0:T(8,128)(2,1)S(1)}, u32[]{:S(2)}, u32[]{:S(2)}) collective-permute-start(bf16[3,192,512]{2,1,0:T(8,128)(2,1)S(1)} %get-tuple-element.39), channel_id=1, source_target_pairs={{0,4},{2,6},{4,0},{6,2},{1,5},{3,7},{5,1},{7,3},{8,12},{10,14},{12... | collective-permute-start | bytes 1769480 | tf_op jit(solution)/shard_map/ppermute | solution.py:132
  28.4 2.8 %collective-permute-start.9 = (bf16[3,192,512]{2,1,0:T(8,128)(2,1)S(1)}, bf16[3,192,512]{2,1,0:T(8,128)(2,1)S(1)}, u32[]{:S(2)}, u32[]{:S(2)}) collective-permute-start(bf16[3,192,512]{2,1,0:T(8,128)(2,1)S(1)} %get-tuple-element.40), channel_id=1, source_target_pairs={{0,6},{2,0},{4,2},{6,4},{1,7},{3,1},{5,3},{7,5},{8,14},{10,8},{12,... | collective-permute-start | bytes 1769480 | tf_op jit(solution)/shard_map/ppermute | solution.py:132
  31.2 2.7 %collective-permute-start.4 = (bf16[192,512]{1,0:T(8,128)(2,1)S(1)}, bf16[192,512]{1,0:T(8,128)(2,1)S(1)}, u32[]{:S(2)}, u32[]{:S(2)}) collective-permute-start(bf16[192,512]{1,0:T(8,128)(2,1)S(1)} %bitcast.49), channel_id=1, source_target_pairs={{0,1},{1,0},{2,3},{3,2},{4,5},{5,4},{6,7},{7,6},{8,9},{9,8},{10,11... | collective-permute-start | bytes 589832 | tf_op jit(solution)/shard_map/ppermute | solution.py:129
  33.9 2.5 %collective-permute-start.5 = (bf16[3,192,512]{2,1,0:T(8,128)(2,1)S(1)}, bf16[3,192,512]{2,1,0:T(8,128)(2,1)S(1)}, u32[]{:S(2)}, u32[]{:S(2)}) collective-permute-start(bf16[3,192,512]{2,1,0:T(8,128)(2,1)S(1)} %get-tuple-element.41), channel_id=1, source_target_pairs={{0,2},{2,4},{4,6},{6,0},{1,3},{3,5},{5,7},{7,1},{8,10},{10,12},{12... | collective-permute-start | bytes 1769480 | tf_op jit(solution)/shard_map/ppermute | solution.py:132
  36.6 4.0 %collective-permute-start.3 = (bf16[3,192,512]{2,1,0:T(8,128)(2,1)S(1)}, bf16[3,192,512]{2,1,0:T(8,128)(2,1)S(1)}, u32[]{:S(2)}, u32[]{:S(2)}) collective-permute-start(bf16[3,192,512]{2,1,0:T(8,128)(2,1)S(1)} %get-tuple-element.46), channel_id=1, source_target_pairs={{0,6},{2,0},{4,2},{6,4},{1,7},{3,1},{5,3},{7,5},{8,14},{10,8},{12,... | collective-permute-start | bytes 1769480 | tf_op jit(solution)/shard_map/ppermute | solution.py:132
  41.9 3.1 %collective-permute-start.1 = (bf16[3,192,512]{2,1,0:T(8,128)(2,1)S(1)}, bf16[3,192,512]{2,1,0:T(8,128)(2,1)S(1)}, u32[]{:S(2)}, u32[]{:S(2)}) collective-permute-start(bf16[3,192,512]{2,1,0:T(8,128)(2,1)S(1)} %get-tuple-element.47), channel_id=1, source_target_pairs={{0,2},{2,4},{4,6},{6,0},{1,3},{3,5},{5,7},{7,1},{8,10},{10,12},{12... | collective-permute-start | bytes 1769480 | tf_op jit(solution)/shard_map/ppermute | solution.py:132
  45.1 9.6 %collective-permute-done.9.refs_7_.refs_11_ = bf16[3,192,512]{2,1,0:T(8,128)(2,1)S(1)} collective-permute-done((bf16[3,192,512]{2,1,0:T(8,128)(2,1)S(1)}, bf16[3,192,512]{2,1,0:T(8,128)(2,1)S(1)}, u32[]{:S(2)}, u32[]{:S(2)}) %collective-permute-start.9) | collective-permute-done | bytes 589856 | tf_op jit(solution)/shard_map/ppermute | solution.py:132
  54.7 3.6 %collective-permute-start.2 = (bf16[3,192,512]{2,1,0:T(8,128)(2,1)S(1)}, bf16[3,192,512]{2,1,0:T(8,128)(2,1)S(1)}, u32[]{:S(2)}, u32[]{:S(2)}) collective-permute-start(bf16[3,192,512]{2,1,0:T(8,128)(2,1)S(1)} %get-tuple-element.48), channel_id=1, source_target_pairs={{0,4},{2,6},{4,0},{6,2},{1,5},{3,7},{5,1},{7,3},{8,12},{10,14},{12... | collective-permute-start | bytes 1769480 | tf_op jit(solution)/shard_map/ppermute | solution.py:132
  58.3 3.8 %collective-permute-start.8 = (bf16[192,512]{1,0:T(8,128)(2,1)S(1)}, bf16[192,512]{1,0:T(8,128)(2,1)S(1)}, u32[]{:S(2)}, u32[]{:S(2)}) collective-permute-start(bf16[192,512]{1,0:T(8,128)(2,1)S(1)} %slice_bitcast_fusion.1), channel_id=1, source_target_pairs={{0,1},{1,0},{2,3},{3,2},{4,5},{5,4},{6,7},{7,6},{8,9},{9,8},{10,11... | collective-permute-start | bytes 589832 | tf_op jit(solution)/shard_map/ppermute | solution.py:129
  64.1 2.4 %collective-permute-start.6 = (bf16[192,512]{1,0:T(8,128)(2,1)S(1)}, bf16[192,512]{1,0:T(8,128)(2,1)S(1)}, u32[]{:S(2)}, u32[]{:S(2)}) collective-permute-start(bf16[192,512]{1,0:T(8,128)(2,1)S(1)} %slice_bitcast_fusion.2), channel_id=1, source_target_pairs={{0,1},{1,0},{2,3},{3,2},{4,5},{5,4},{6,7},{7,6},{8,9},{9,8},{10,11... | collective-permute-start | bytes 589832 | tf_op jit(solution)/shard_map/ppermute | solution.py:129
  69.4 4.7 %collective-permute-start.17 = (bf16[512,512]{1,0:T(8,128)(2,1)}, bf16[512,512]{1,0:T(8,128)(2,1)}, u32[]{:S(2)}, u32[]{:S(2)}) collective-permute-start(bf16[512,512]{1,0:T(8,128)(2,1)} %shard_map.68), channel_id=1, source_target_pairs={{0,8},{8,0},{1,9},{9,1},{2,10},{10,2},{3,11},{11,3},{4,12},{12,4},... | collective-permute-start | bytes 1572872 | tf_op jit(solution)/shard_map/ppermute | solution.py:158
  74.2 5.7 %collective-permute-done.2.refs_10_.refs_6_ = bf16[3,192,512]{2,1,0:T(8,128)(2,1)S(1)} collective-permute-done((bf16[3,192,512]{2,1,0:T(8,128)(2,1)S(1)}, bf16[3,192,512]{2,1,0:T(8,128)(2,1)S(1)}, u32[]{:S(2)}, u32[]{:S(2)}) %collective-permute-start.2) | collective-permute-done | bytes 589856 | tf_op jit(solution)/shard_map/ppermute | solution.py:132
  82.7 2.8 %collective-permute-start.16 = (bf16[256,1024]{1,0:T(8,128)(2,1)}, bf16[256,1024]{1,0:T(8,128)(2,1)}, u32[]{:S(2)}, u32[]{:S(2)}) collective-permute-start(bf16[256,1024]{1,0:T(8,128)(2,1)} %constant_dynamic-slice_fusion), channel_id=1, source_target_pairs={{0,1},{1,0},{2,3},{3,2},{4,5},{5,4},{6,7},{7,6},{8,9},{9,8},{10,11... | collective-permute-start | bytes 1572872 | tf_op jit(solution)/shard_map/ppermute | solution.py:129
  88.2 2.4 %collective-permute-start.13 = (bf16[192,512]{1,0:T(8,128)(2,1)S(1)}, bf16[192,512]{1,0:T(8,128)(2,1)S(1)}, u32[]{:S(2)}, u32[]{:S(2)}) collective-permute-start(bf16[192,512]{1,0:T(8,128)(2,1)S(1)} %slice_bitcast_fusion.8), channel_id=1, source_target_pairs={{0,1},{1,0},{2,3},{3,2},{4,5},{5,4},{6,7},{7,6},{8,9},{9,8},{10,11... | collective-permute-start | bytes 589832 | tf_op jit(solution)/shard_map/ppermute | solution.py:129
  93.2 2.4 %collective-permute-start.11 = (bf16[192,512]{1,0:T(8,128)(2,1)}, bf16[192,512]{1,0:T(8,128)(2,1)}, u32[]{:S(2)}, u32[]{:S(2)}) collective-permute-start(bf16[192,512]{1,0:T(8,128)(2,1)} %slice_bitcast_fusion.10), channel_id=1, source_target_pairs={{0,1},{1,0},{2,3},{3,2},{4,5},{5,4},{6,7},{7,6},{8,9},{9,8},{10,11... | collective-permute-start | bytes 589832 | tf_op jit(solution)/shard_map/ppermute | solution.py:129
  96.3 4.8 %collective-permute-start.15 = (bf16[512,512]{1,0:T(8,128)(2,1)}, bf16[512,512]{1,0:T(8,128)(2,1)}, u32[]{:S(2)}, u32[]{:S(2)}) collective-permute-start(bf16[512,512]{1,0:T(8,128)(2,1)} %shard_map.69), channel_id=1, source_target_pairs={{0,8},{8,0},{1,9},{9,1},{2,10},{10,2},{3,11},{11,3},{4,12},{12,4},... | collective-permute-start | bytes 1572872 | tf_op jit(solution)/shard_map/ppermute | solution.py:158
  108.4 2.0 %shard_map.71.own_ref = f32[512,512]{1,0:T(8,128)S(1)} custom-call(bf16[192,512]{1,0:T(8,128)(2,1)} %collective-permute-done.11.refs_0_, bf16[192,512]{1,0:T(8,128)(2,1)} %collective-permute-done.12.refs_1_, bf16[192,512]{1,0:T(8,128)(2,1)S(1)} %copy-done.17, bf16[192,512]{1,0:T(8,128)(2,1)S(1)} %collective-permute-done.14.refs_3_, ...), custom_call_target="tpu_custom_call" | custom-call | flops 1 | bytes 1 | tf_op jit(solution)/shard_map/pallas_call | solution.py:43
  110.5 2.4 %shard_map.70.refs_0_ = f32[512,512]{1,0:T(8,128)S(1)} custom-call(bf16[192,512]{1,0:T(8,128)(2,1)} %collective-permute-done.11.refs_0_, bf16[192,512]{1,0:T(8,128)(2,1)} %collective-permute-done.12.refs_1_, bf16[192,512]{1,0:T(8,128)(2,1)S(1)} %copy-done.17, bf16[192,512]{1,0:T(8,128)(2,1)S(1)} %collective-permute-done.14.refs_3_, ...), custom_call_target="tpu_custom_call" | custom-call | flops 1 | bytes 1 | tf_op jit(solution)/shard_map/pallas_call | solution.py:43
  116.0 3.0 %shard_map.72.refs_4_ = bf16[4,8,2,64,128]{4,3,2,1,0:T(8,128)(2,1)S(1)} custom-call(f32[512,512]{1,0:T(8,128)S(1)} %copy-done.15, bf16[512,512]{1,0:T(8,128)(2,1)} %collective-permute-done.17.part_ref, bf16[512,1024]{1,0:T(8,128)(2,1)S(1)} %pad_maximum_fusion.local_ref.refs_2_, f32[4,8,2,8,1024]{4,3,2,1,0:T(8,128)S(1)} %bitcast.39), custom_call_target="tpu_custom_call" | custom-call | flops 1 | bytes 1 | tf_op jit(solution)/shard_map/pallas_call | solution.py:88
  119.0 2.9 %shard_map.73 = bf16[4,8,2,64,128]{4,3,2,1,0:T(8,128)(2,1)S(1)} custom-call(f32[512,512]{1,0:T(8,128)S(1)} %copy-done.13, bf16[512,512]{1,0:T(8,128)(2,1)} %collective-permute-done.15.refs_1_, bf16[512,1024]{1,0:T(8,128)(2,1)S(1)} %pad_maximum_fusion.local_ref.refs_2_, f32[4,8,2,8,1024]{4,3,2,1,0:T(8,128)S(1)} %bitcast.40, ...), custom_call_target="tpu_custom_call", output_to_operand_aliasing={{}: (4, {})} | custom-call | flops 1 | bytes 1 | tf_op jit(solution)/shard_map/pallas_call | solution.py:88
  122.0 47.9 %all_to_all.10 = bf16[64,64,128]{2,1,0:T(8,128)(2,1)S(1)} all-to-all(bf16[64,64,128]{2,1,0:T(8,128)(2,1)S(1)} %bitcast.41), channel_id=1, replica_groups=mesh['ylo'=4,'z'=8,'yhi'=2,'x'=4,'c'=2] {'ylo','z','c'}, dimensions={0} | all-to-all | bytes 2097152 | tf_op jit(solution)/shard_map/all_to_all | solution.py:135
  (85 shorter events, 28.8 us)
Async XLA Ops:
  3.1 111.7 %all-to-all-start = ((f32[64,8,1024]{2,1,0:T(8,128)}), f32[64,8,1024]{2,1,0:T(8,128)S(1)}, u32[]{:S(2)}, u32[]{:S(2)}) async-start(f32[64,8,1024]{2,1,0:T(8,128)} %bitcast.46), calls=%async_computation | async-start | bytes 4194304 | tf_op jit(solution)/shard_map/all_to_all | solution.py:135
  19.5 4.0 %collective-permute-start = (bf16[192,1024]{1,0:T(8,128)(2,1)}, bf16[192,1024]{1,0:T(8,128)(2,1)S(1)}, u32[]{:S(2)}, u32[]{:S(2)}) collective-permute-start(bf16[192,1024]{1,0:T(8,128)(2,1)} %get-tuple-element.37), channel_id=1, source_target_pairs={{0,1},{1,0},{2,3},{3,2},{4,5},{5,4},{6,7},{7,6},{8,9},{9,8},{10,11... | collective-permute-start | bytes 1179656 | tf_op jit(solution)/shard_map/ppermute | solution.py:129
  23.8 18.2 %collective-permute-start.7 = (bf16[3,192,512]{2,1,0:T(8,128)(2,1)S(1)}, bf16[3,192,512]{2,1,0:T(8,128)(2,1)S(1)}, u32[]{:S(2)}, u32[]{:S(2)}) collective-permute-start(bf16[3,192,512]{2,1,0:T(8,128)(2,1)S(1)} %get-tuple-element.39), channel_id=1, source_target_pairs={{0,4},{2,6},{4,0},{6,2},{1,5},{3,7},{5,1},{7,3},{8,12},{10,14},{12... | collective-permute-start | bytes 1769480 | tf_op jit(solution)/shard_map/ppermute | solution.py:132
  28.4 26.2 %collective-permute-start.9 = (bf16[3,192,512]{2,1,0:T(8,128)(2,1)S(1)}, bf16[3,192,512]{2,1,0:T(8,128)(2,1)S(1)}, u32[]{:S(2)}, u32[]{:S(2)}) collective-permute-start(bf16[3,192,512]{2,1,0:T(8,128)(2,1)S(1)} %get-tuple-element.40), channel_id=1, source_target_pairs={{0,6},{2,0},{4,2},{6,4},{1,7},{3,1},{5,3},{7,5},{8,14},{10,8},{12,... | collective-permute-start | bytes 1769480 | tf_op jit(solution)/shard_map/ppermute | solution.py:132
  31.2 31.0 %collective-permute-start.4 = (bf16[192,512]{1,0:T(8,128)(2,1)S(1)}, bf16[192,512]{1,0:T(8,128)(2,1)S(1)}, u32[]{:S(2)}, u32[]{:S(2)}) collective-permute-start(bf16[192,512]{1,0:T(8,128)(2,1)S(1)} %bitcast.49), channel_id=1, source_target_pairs={{0,1},{1,0},{2,3},{3,2},{4,5},{5,4},{6,7},{7,6},{8,9},{9,8},{10,11... | collective-permute-start | bytes 589832 | tf_op jit(solution)/shard_map/ppermute | solution.py:129
  33.9 24.4 %collective-permute-start.5 = (bf16[3,192,512]{2,1,0:T(8,128)(2,1)S(1)}, bf16[3,192,512]{2,1,0:T(8,128)(2,1)S(1)}, u32[]{:S(2)}, u32[]{:S(2)}) collective-permute-start(bf16[3,192,512]{2,1,0:T(8,128)(2,1)S(1)} %get-tuple-element.41), channel_id=1, source_target_pairs={{0,2},{2,4},{4,6},{6,0},{1,3},{3,5},{5,7},{7,1},{8,10},{10,12},{12... | collective-permute-start | bytes 1769480 | tf_op jit(solution)/shard_map/ppermute | solution.py:132
  36.6 37.5 %collective-permute-start.3 = (bf16[3,192,512]{2,1,0:T(8,128)(2,1)S(1)}, bf16[3,192,512]{2,1,0:T(8,128)(2,1)S(1)}, u32[]{:S(2)}, u32[]{:S(2)}) collective-permute-start(bf16[3,192,512]{2,1,0:T(8,128)(2,1)S(1)} %get-tuple-element.46), channel_id=1, source_target_pairs={{0,6},{2,0},{4,2},{6,4},{1,7},{3,1},{5,3},{7,5},{8,14},{10,8},{12,... | collective-permute-start | bytes 1769480 | tf_op jit(solution)/shard_map/ppermute | solution.py:132
  41.9 38.0 %copy-start = (bf16[3,192,512]{2,1,0:T(8,128)(2,1)}, bf16[3,192,512]{2,1,0:T(8,128)(2,1)S(1)}, u32[]{:S(2)}) copy-start(bf16[3,192,512]{2,1,0:T(8,128)(2,1)S(1)} %collective-permute-done.7.refs_6_.refs_10_) | copy-start | bytes 1769476
  41.9 32.3 %collective-permute-start.1 = (bf16[3,192,512]{2,1,0:T(8,128)(2,1)S(1)}, bf16[3,192,512]{2,1,0:T(8,128)(2,1)S(1)}, u32[]{:S(2)}, u32[]{:S(2)}) collective-permute-start(bf16[3,192,512]{2,1,0:T(8,128)(2,1)S(1)} %get-tuple-element.47), channel_id=1, source_target_pairs={{0,2},{2,4},{4,6},{6,0},{1,3},{3,5},{5,7},{7,1},{8,10},{10,12},{12... | collective-permute-start | bytes 1769480 | tf_op jit(solution)/shard_map/ppermute | solution.py:132
  54.7 25.3 %copy-start.2 = (bf16[3,192,512]{2,1,0:T(8,128)(2,1)}, bf16[3,192,512]{2,1,0:T(8,128)(2,1)S(1)}, u32[]{:S(2)}) copy-start(bf16[3,192,512]{2,1,0:T(8,128)(2,1)S(1)} %collective-permute-done.9.refs_7_.refs_11_) | copy-start | bytes 1769476
  54.7 25.3 %collective-permute-start.2 = (bf16[3,192,512]{2,1,0:T(8,128)(2,1)S(1)}, bf16[3,192,512]{2,1,0:T(8,128)(2,1)S(1)}, u32[]{:S(2)}, u32[]{:S(2)}) collective-permute-start(bf16[3,192,512]{2,1,0:T(8,128)(2,1)S(1)} %get-tuple-element.48), channel_id=1, source_target_pairs={{0,4},{2,6},{4,0},{6,2},{1,5},{3,7},{5,1},{7,3},{8,12},{10,14},{12... | collective-permute-start | bytes 1769480 | tf_op jit(solution)/shard_map/ppermute | solution.py:132
  58.3 21.6 %copy-start.4 = (bf16[3,192,512]{2,1,0:T(8,128)(2,1)}, bf16[3,192,512]{2,1,0:T(8,128)(2,1)S(1)}, u32[]{:S(2)}) copy-start(bf16[3,192,512]{2,1,0:T(8,128)(2,1)S(1)} %collective-permute-done.5.refs_5_.refs_9_) | copy-start | bytes 1769476
  58.3 5.8 %collective-permute-start.8 = (bf16[192,512]{1,0:T(8,128)(2,1)S(1)}, bf16[192,512]{1,0:T(8,128)(2,1)S(1)}, u32[]{:S(2)}, u32[]{:S(2)}) collective-permute-start(bf16[192,512]{1,0:T(8,128)(2,1)S(1)} %slice_bitcast_fusion.1), channel_id=1, source_target_pairs={{0,1},{1,0},{2,3},{3,2},{4,5},{5,4},{6,7},{7,6},{8,9},{9,8},{10,11... | collective-permute-start | bytes 589832 | tf_op jit(solution)/shard_map/ppermute | solution.py:129
  62.2 4.4 %collective-permute-start.10 = (bf16[192,512]{1,0:T(8,128)(2,1)S(1)}, bf16[192,512]{1,0:T(8,128)(2,1)S(1)}, u32[]{:S(2)}, u32[]{:S(2)}) collective-permute-start(bf16[192,512]{1,0:T(8,128)(2,1)S(1)} %slice_bitcast_fusion), channel_id=1, source_target_pairs={{0,1},{1,0},{2,3},{3,2},{4,5},{5,4},{6,7},{7,6},{8,9},{9,8},{10,11... | collective-permute-start | bytes 589832 | tf_op jit(solution)/shard_map/ppermute | solution.py:129
  64.1 3.5 %collective-permute-start.6 = (bf16[192,512]{1,0:T(8,128)(2,1)S(1)}, bf16[192,512]{1,0:T(8,128)(2,1)S(1)}, u32[]{:S(2)}, u32[]{:S(2)}) collective-permute-start(bf16[192,512]{1,0:T(8,128)(2,1)S(1)} %slice_bitcast_fusion.2), channel_id=1, source_target_pairs={{0,1},{1,0},{2,3},{3,2},{4,5},{5,4},{6,7},{7,6},{8,9},{9,8},{10,11... | collective-permute-start | bytes 589832 | tf_op jit(solution)/shard_map/ppermute | solution.py:129
  69.4 43.5 %collective-permute-start.17 = (bf16[512,512]{1,0:T(8,128)(2,1)}, bf16[512,512]{1,0:T(8,128)(2,1)}, u32[]{:S(2)}, u32[]{:S(2)}) collective-permute-start(bf16[512,512]{1,0:T(8,128)(2,1)} %shard_map.68), channel_id=1, source_target_pairs={{0,8},{8,0},{1,9},{9,1},{2,10},{10,2},{3,11},{11,3},{4,12},{12,4},... | collective-permute-start | bytes 1572872 | tf_op jit(solution)/shard_map/ppermute | solution.py:158
  82.7 30.3 %collective-permute-start.16 = (bf16[256,1024]{1,0:T(8,128)(2,1)}, bf16[256,1024]{1,0:T(8,128)(2,1)}, u32[]{:S(2)}, u32[]{:S(2)}) collective-permute-start(bf16[256,1024]{1,0:T(8,128)(2,1)} %constant_dynamic-slice_fusion), channel_id=1, source_target_pairs={{0,1},{1,0},{2,3},{3,2},{4,5},{5,4},{6,7},{7,6},{8,9},{9,8},{10,11... | collective-permute-start | bytes 1572872 | tf_op jit(solution)/shard_map/ppermute | solution.py:129
  86.3 7.0 %collective-permute-start.14 = (bf16[192,512]{1,0:T(8,128)(2,1)S(1)}, bf16[192,512]{1,0:T(8,128)(2,1)S(1)}, u32[]{:S(2)}, u32[]{:S(2)}) collective-permute-start(bf16[192,512]{1,0:T(8,128)(2,1)S(1)} %slice_bitcast_fusion.7), channel_id=1, source_target_pairs={{0,1},{1,0},{2,3},{3,2},{4,5},{5,4},{6,7},{7,6},{8,9},{9,8},{10,11... | collective-permute-start | bytes 589832 | tf_op jit(solution)/shard_map/ppermute | solution.py:129
  88.2 7.5 %collective-permute-start.13 = (bf16[192,512]{1,0:T(8,128)(2,1)S(1)}, bf16[192,512]{1,0:T(8,128)(2,1)S(1)}, u32[]{:S(2)}, u32[]{:S(2)}) collective-permute-start(bf16[192,512]{1,0:T(8,128)(2,1)S(1)} %slice_bitcast_fusion.8), channel_id=1, source_target_pairs={{0,1},{1,0},{2,3},{3,2},{4,5},{5,4},{6,7},{7,6},{8,9},{9,8},{10,11... | collective-permute-start | bytes 589832 | tf_op jit(solution)/shard_map/ppermute | solution.py:129
  90.6 10.5 %collective-permute-start.12 = (bf16[192,512]{1,0:T(8,128)(2,1)}, bf16[192,512]{1,0:T(8,128)(2,1)}, u32[]{:S(2)}, u32[]{:S(2)}) collective-permute-start(bf16[192,512]{1,0:T(8,128)(2,1)} %slice_bitcast_fusion.9), channel_id=1, source_target_pairs={{0,1},{1,0},{2,3},{3,2},{4,5},{5,4},{6,7},{7,6},{8,9},{9,8},{10,11... | collective-permute-start | bytes 589832 | tf_op jit(solution)/shard_map/ppermute | solution.py:129
  93.2 7.9 %collective-permute-start.11 = (bf16[192,512]{1,0:T(8,128)(2,1)}, bf16[192,512]{1,0:T(8,128)(2,1)}, u32[]{:S(2)}, u32[]{:S(2)}) collective-permute-start(bf16[192,512]{1,0:T(8,128)(2,1)} %slice_bitcast_fusion.10), channel_id=1, source_target_pairs={{0,1},{1,0},{2,3},{3,2},{4,5},{5,4},{6,7},{7,6},{8,9},{9,8},{10,11... | collective-permute-start | bytes 589832 | tf_op jit(solution)/shard_map/ppermute | solution.py:129
  96.3 22.6 %collective-permute-start.15 = (bf16[512,512]{1,0:T(8,128)(2,1)}, bf16[512,512]{1,0:T(8,128)(2,1)}, u32[]{:S(2)}, u32[]{:S(2)}) collective-permute-start(bf16[512,512]{1,0:T(8,128)(2,1)} %shard_map.69), channel_id=1, source_target_pairs={{0,8},{8,0},{1,9},{9,1},{2,10},{10,2},{3,11},{11,3},{4,12},{12,4},... | collective-permute-start | bytes 1572872 | tf_op jit(solution)/shard_map/ppermute | solution.py:158
  121.9 47.9 %copy-start.18 = (f32[1,8,2048]{2,1,0:T(8,128)S(1)}, f32[1,8,2048]{2,1,0:T(8,128)}, u32[]{:S(2)}) copy-start(f32[1,8,2048]{2,1,0:T(8,128)} %param.8) | copy-start | bytes 196612
  121.9 47.9 %copy-start.19 = (f32[1,8,2048]{2,1,0:T(8,128)S(1)}, f32[1,8,2048]{2,1,0:T(8,128)}, u32[]{:S(2)}) copy-start(f32[1,8,2048]{2,1,0:T(8,128)} %param.9) | copy-start | bytes 196612
  (18 other events, 65.9 us)

commit v5 on v4

--- a/solution.py
+++ b/solution.py
@@ -20,7 +20,7 @@
 HALF = W2 // 2
 CHUNK = HALF // 2
 BLOCKS = CHUNK // 128
-WIDE = 2
+WIDE = 4
 ROWS = 512
 INV = 1.0 / math.sqrt(TOK * 16)
 
@@ -92,7 +92,7 @@
         in_specs=specs,
         out_specs=out_tile,
         input_output_aliases=aliases,
-        compiler_params=pltpu.CompilerParams(vmem_limit_bytes=6 * 1024 * 1024),
+        compiler_params=pltpu.CompilerParams(vmem_limit_bytes=10 * 1024 * 1024),
         cost_estimate=COST,
     )(*operands)
 

time: 172 us -> 171 us (level)
  no operation moved by 1% of the time
where the time goes in v5:
time: 171 us; the launch traced here: 170 us
  starting transfers between devices  70.3 us (41%)
  blocking collectives  48.6 us (28%)
  waiting for transfers between devices  17.7 us (10%)
  local copies, waits for them, and re-layouts  16.5 us (10%)
  Pallas kernels  13.4 us (8%)
  other arithmetic  2.13 us (1%)
    all_to_all x1, blocking collectives, all_to_all(): return lax.all_to_all(array, axes, 0, 0, tiled=True)  48.6 us
    ppermute x10, starting transfers between devices, other_core(): return lax.ppermute(array, 'c', shift(2, 1))  24.6 us
    ppermute x6, starting transfers between devices, along_x(): return lax.ppermute(array, 'x', shift(X, k))  20.6 us
    ppermute x6, waiting for transfers between devices, along_x(): return lax.ppermute(array, 'x', shift(X, k))  16.6 us
    all_to_all x1, starting transfers between devices, all_to_all(): return lax.all_to_all(array, axes, 0, 0, tiled=True)  15.5 us
    ppermute x2, starting transfers between devices, body(): far = [lax.ppermute(part, 'yhi', shift(2, 1)) for part in sent_far]  9.5 us
    unnamed x46, local copies, waits for them, and re-layouts  9.25 us
    pallas_call x4, Pallas kernels, matmul(): pl.pallas_call(matmul_kernel, out_shape=jax.ShapeDtypeStruct((ROWS, CHUNK...  8.09 us
  transfers between devices with their start and end apart: 19, of which 4 were waited for; matrix products, arithmetic and copies ran while one was open for 4% of the time, Pallas kernels for 6%

profile of v5, /device:TPU:1, one launch (start us, length us, event | category | flops | bytes accessed | tf_op | source)
XLA Modules:
  0.0 170.0 jit_solution(15331945108481921828)
XLA Ops:
  0.6 2.4 %broadcast_in_dim.12 = f32[32,2,8,1024]{3,2,1,0:T(8,128)} broadcast(f32[2,8,1024]{2,1,0:T(8,128)} %bitcast.43), dimensions={1,2,3} | broadcast | bytes 2162688 | tf_op jit(solution)/shard_map/broadcast_in_dim | solution.py:168
  3.1 15.5 %all-to-all-start = ((f32[64,8,1024]{2,1,0:T(8,128)}), f32[64,8,1024]{2,1,0:T(8,128)S(1)}, u32[]{:S(2)}, u32[]{:S(2)}) async-start(f32[64,8,1024]{2,1,0:T(8,128)} %bitcast.46), calls=%async_computation | async-start | bytes 4194304 | tf_op jit(solution)/shard_map/all_to_all | solution.py:135
  19.5 2.4 %collective-permute-start = (bf16[192,1024]{1,0:T(8,128)(2,1)}, bf16[192,1024]{1,0:T(8,128)(2,1)S(1)}, u32[]{:S(2)}, u32[]{:S(2)}) collective-permute-start(bf16[192,1024]{1,0:T(8,128)(2,1)} %get-tuple-element.37), channel_id=1, source_target_pairs={{0,1},{1,0},{2,3},{3,2},{4,5},{5,4},{6,7},{7,6},{8,9},{9,8},{10,11... | collective-permute-start | bytes 1179656 | tf_op jit(solution)/shard_map/ppermute | solution.py:129
  23.8 4.7 %collective-permute-start.7 = (bf16[3,192,512]{2,1,0:T(8,128)(2,1)S(1)}, bf16[3,192,512]{2,1,0:T(8,128)(2,1)S(1)}, u32[]{:S(2)}, u32[]{:S(2)}) collective-permute-start(bf16[3,192,512]{2,1,0:T(8,128)(2,1)S(1)} %get-tuple-element.39), channel_id=1, source_target_pairs={{0,4},{2,6},{4,0},{6,2},{1,5},{3,7},{5,1},{7,3},{8,12},{10,14},{12... | collective-permute-start | bytes 1769480 | tf_op jit(solution)/shard_map/ppermute | solution.py:132
  28.4 2.8 %collective-permute-start.9 = (bf16[3,192,512]{2,1,0:T(8,128)(2,1)S(1)}, bf16[3,192,512]{2,1,0:T(8,128)(2,1)S(1)}, u32[]{:S(2)}, u32[]{:S(2)}) collective-permute-start(bf16[3,192,512]{2,1,0:T(8,128)(2,1)S(1)} %get-tuple-element.40), channel_id=1, source_target_pairs={{0,6},{2,0},{4,2},{6,4},{1,7},{3,1},{5,3},{7,5},{8,14},{10,8},{12,... | collective-permute-start | bytes 1769480 | tf_op jit(solution)/shard_map/ppermute | solution.py:132
  31.2 2.7 %collective-permute-start.4 = (bf16[192,512]{1,0:T(8,128)(2,1)S(1)}, bf16[192,512]{1,0:T(8,128)(2,1)S(1)}, u32[]{:S(2)}, u32[]{:S(2)}) collective-permute-start(bf16[192,512]{1,0:T(8,128)(2,1)S(1)} %bitcast.49), channel_id=1, source_target_pairs={{0,1},{1,0},{2,3},{3,2},{4,5},{5,4},{6,7},{7,6},{8,9},{9,8},{10,11... | collective-permute-start | bytes 589832 | tf_op jit(solution)/shard_map/ppermute | solution.py:129
  33.9 2.5 %collective-permute-start.5 = (bf16[3,192,512]{2,1,0:T(8,128)(2,1)S(1)}, bf16[3,192,512]{2,1,0:T(8,128)(2,1)S(1)}, u32[]{:S(2)}, u32[]{:S(2)}) collective-permute-start(bf16[3,192,512]{2,1,0:T(8,128)(2,1)S(1)} %get-tuple-element.41), channel_id=1, source_target_pairs={{0,2},{2,4},{4,6},{6,0},{1,3},{3,5},{5,7},{7,1},{8,10},{10,12},{12... | collective-permute-start | bytes 1769480 | tf_op jit(solution)/shard_map/ppermute | solution.py:132
  36.6 4.0 %collective-permute-start.3 = (bf16[3,192,512]{2,1,0:T(8,128)(2,1)S(1)}, bf16[3,192,512]{2,1,0:T(8,128)(2,1)S(1)}, u32[]{:S(2)}, u32[]{:S(2)}) collective-permute-start(bf16[3,192,512]{2,1,0:T(8,128)(2,1)S(1)} %get-tuple-element.46), channel_id=1, source_target_pairs={{0,6},{2,0},{4,2},{6,4},{1,7},{3,1},{5,3},{7,5},{8,14},{10,8},{12,... | collective-permute-start | bytes 1769480 | tf_op jit(solution)/shard_map/ppermute | solution.py:132
  41.9 3.1 %collective-permute-start.1 = (bf16[3,192,512]{2,1,0:T(8,128)(2,1)S(1)}, bf16[3,192,512]{2,1,0:T(8,128)(2,1)S(1)}, u32[]{:S(2)}, u32[]{:S(2)}) collective-permute-start(bf16[3,192,512]{2,1,0:T(8,128)(2,1)S(1)} %get-tuple-element.47), channel_id=1, source_target_pairs={{0,2},{2,4},{4,6},{6,0},{1,3},{3,5},{5,7},{7,1},{8,10},{10,12},{12... | collective-permute-start | bytes 1769480 | tf_op jit(solution)/shard_map/ppermute | solution.py:132
  45.1 9.6 %collective-permute-done.9.refs_7_.refs_11_ = bf16[3,192,512]{2,1,0:T(8,128)(2,1)S(1)} collective-permute-done((bf16[3,192,512]{2,1,0:T(8,128)(2,1)S(1)}, bf16[3,192,512]{2,1,0:T(8,128)(2,1)S(1)}, u32[]{:S(2)}, u32[]{:S(2)}) %collective-permute-start.9) | collective-permute-done | bytes 589856 | tf_op jit(solution)/shard_map/ppermute | solution.py:132
  54.7 3.6 %collective-permute-start.2 = (bf16[3,192,512]{2,1,0:T(8,128)(2,1)S(1)}, bf16[3,192,512]{2,1,0:T(8,128)(2,1)S(1)}, u32[]{:S(2)}, u32[]{:S(2)}) collective-permute-start(bf16[3,192,512]{2,1,0:T(8,128)(2,1)S(1)} %get-tuple-element.48), channel_id=1, source_target_pairs={{0,4},{2,6},{4,0},{6,2},{1,5},{3,7},{5,1},{7,3},{8,12},{10,14},{12... | collective-permute-start | bytes 1769480 | tf_op jit(solution)/shard_map/ppermute | solution.py:132
  58.3 3.8 %collective-permute-start.8 = (bf16[192,512]{1,0:T(8,128)(2,1)S(1)}, bf16[192,512]{1,0:T(8,128)(2,1)S(1)}, u32[]{:S(2)}, u32[]{:S(2)}) collective-permute-start(bf16[192,512]{1,0:T(8,128)(2,1)S(1)} %slice_bitcast_fusion.1), channel_id=1, source_target_pairs={{0,1},{1,0},{2,3},{3,2},{4,5},{5,4},{6,7},{7,6},{8,9},{9,8},{10,11... | collective-permute-start | bytes 589832 | tf_op jit(solution)/shard_map/ppermute | solution.py:129
  64.1 2.4 %collective-permute-start.6 = (bf16[192,512]{1,0:T(8,128)(2,1)S(1)}, bf16[192,512]{1,0:T(8,128)(2,1)S(1)}, u32[]{:S(2)}, u32[]{:S(2)}) collective-permute-start(bf16[192,512]{1,0:T(8,128)(2,1)S(1)} %slice_bitcast_fusion.2), channel_id=1, source_target_pairs={{0,1},{1,0},{2,3},{3,2},{4,5},{5,4},{6,7},{7,6},{8,9},{9,8},{10,11... | collective-permute-start | bytes 589832 | tf_op jit(solution)/shard_map/ppermute | solution.py:129
  69.4 4.7 %collective-permute-start.17 = (bf16[512,512]{1,0:T(8,128)(2,1)}, bf16[512,512]{1,0:T(8,128)(2,1)}, u32[]{:S(2)}, u32[]{:S(2)}) collective-permute-start(bf16[512,512]{1,0:T(8,128)(2,1)} %shard_map.68), channel_id=1, source_target_pairs={{0,8},{8,0},{1,9},{9,1},{2,10},{10,2},{3,11},{11,3},{4,12},{12,4},... | collective-permute-start | bytes 1572872 | tf_op jit(solution)/shard_map/ppermute | solution.py:158
  74.2 5.7 %collective-permute-done.2.refs_10_.refs_6_ = bf16[3,192,512]{2,1,0:T(8,128)(2,1)S(1)} collective-permute-done((bf16[3,192,512]{2,1,0:T(8,128)(2,1)S(1)}, bf16[3,192,512]{2,1,0:T(8,128)(2,1)S(1)}, u32[]{:S(2)}, u32[]{:S(2)}) %collective-permute-start.2) | collective-permute-done | bytes 589856 | tf_op jit(solution)/shard_map/ppermute | solution.py:132
  82.7 2.8 %collective-permute-start.16 = (bf16[256,1024]{1,0:T(8,128)(2,1)}, bf16[256,1024]{1,0:T(8,128)(2,1)}, u32[]{:S(2)}, u32[]{:S(2)}) collective-permute-start(bf16[256,1024]{1,0:T(8,128)(2,1)} %constant_dynamic-slice_fusion), channel_id=1, source_target_pairs={{0,1},{1,0},{2,3},{3,2},{4,5},{5,4},{6,7},{7,6},{8,9},{9,8},{10,11... | collective-permute-start | bytes 1572872 | tf_op jit(solution)/shard_map/ppermute | solution.py:129
  88.2 2.4 %collective-permute-start.13 = (bf16[192,512]{1,0:T(8,128)(2,1)S(1)}, bf16[192,512]{1,0:T(8,128)(2,1)S(1)}, u32[]{:S(2)}, u32[]{:S(2)}) collective-permute-start(bf16[192,512]{1,0:T(8,128)(2,1)S(1)} %slice_bitcast_fusion.8), channel_id=1, source_target_pairs={{0,1},{1,0},{2,3},{3,2},{4,5},{5,4},{6,7},{7,6},{8,9},{9,8},{10,11... | collective-permute-start | bytes 589832 | tf_op jit(solution)/shard_map/ppermute | solution.py:129
  93.2 2.4 %collective-permute-start.11 = (bf16[192,512]{1,0:T(8,128)(2,1)}, bf16[192,512]{1,0:T(8,128)(2,1)}, u32[]{:S(2)}, u32[]{:S(2)}) collective-permute-start(bf16[192,512]{1,0:T(8,128)(2,1)} %slice_bitcast_fusion.10), channel_id=1, source_target_pairs={{0,1},{1,0},{2,3},{3,2},{4,5},{5,4},{6,7},{7,6},{8,9},{9,8},{10,11... | collective-permute-start | bytes 589832 | tf_op jit(solution)/shard_map/ppermute | solution.py:129
  96.3 4.8 %collective-permute-start.15 = (bf16[512,512]{1,0:T(8,128)(2,1)}, bf16[512,512]{1,0:T(8,128)(2,1)}, u32[]{:S(2)}, u32[]{:S(2)}) collective-permute-start(bf16[512,512]{1,0:T(8,128)(2,1)} %shard_map.69), channel_id=1, source_target_pairs={{0,8},{8,0},{1,9},{9,1},{2,10},{10,2},{3,11},{11,3},{4,12},{12,4},... | collective-permute-start | bytes 1572872 | tf_op jit(solution)/shard_map/ppermute | solution.py:158
  108.4 2.0 %shard_map.71.own_ref = f32[512,512]{1,0:T(8,128)S(1)} custom-call(bf16[192,512]{1,0:T(8,128)(2,1)} %collective-permute-done.11.refs_0_, bf16[192,512]{1,0:T(8,128)(2,1)} %collective-permute-done.12.refs_1_, bf16[192,512]{1,0:T(8,128)(2,1)S(1)} %copy-done.17, bf16[192,512]{1,0:T(8,128)(2,1)S(1)} %collective-permute-done.14.refs_3_, ...), custom_call_target="tpu_custom_call" | custom-call | flops 1 | bytes 1 | tf_op jit(solution)/shard_map/pallas_call | solution.py:43
  110.5 2.4 %shard_map.70.refs_0_ = f32[512,512]{1,0:T(8,128)S(1)} custom-call(bf16[192,512]{1,0:T(8,128)(2,1)} %collective-permute-done.11.refs_0_, bf16[192,512]{1,0:T(8,128)(2,1)} %collective-permute-done.12.refs_1_, bf16[192,512]{1,0:T(8,128)(2,1)S(1)} %copy-done.17, bf16[192,512]{1,0:T(8,128)(2,1)S(1)} %collective-permute-done.14.refs_3_, ...), custom_call_target="tpu_custom_call" | custom-call | flops 1 | bytes 1 | tf_op jit(solution)/shard_map/pallas_call | solution.py:43
  116.0 2.3 %shard_map.72.refs_4_ = bf16[4,8,2,64,128]{4,3,2,1,0:T(8,128)(2,1)S(1)} custom-call(f32[512,512]{1,0:T(8,128)S(1)} %copy-done.15, bf16[512,512]{1,0:T(8,128)(2,1)} %collective-permute-done.17.part_ref, bf16[512,1024]{1,0:T(8,128)(2,1)S(1)} %pad_maximum_fusion.local_ref.refs_2_, f32[4,8,2,8,1024]{4,3,2,1,0:T(8,128)S(1)} %bitcast.39), custom_call_target="tpu_custom_call" | custom-call | flops 1 | bytes 1 | tf_op jit(solution)/shard_map/pallas_call | solution.py:88
  118.3 2.2 %shard_map.73 = bf16[4,8,2,64,128]{4,3,2,1,0:T(8,128)(2,1)S(1)} custom-call(f32[512,512]{1,0:T(8,128)S(1)} %copy-done.13, bf16[512,512]{1,0:T(8,128)(2,1)} %collective-permute-done.15.refs_1_, bf16[512,1024]{1,0:T(8,128)(2,1)S(1)} %pad_maximum_fusion.local_ref.refs_2_, f32[4,8,2,8,1024]{4,3,2,1,0:T(8,128)S(1)} %bitcast.40, ...), custom_call_target="tpu_custom_call", output_to_operand_aliasing={{}: (4, {})} | custom-call | flops 1 | bytes 1 | tf_op jit(solution)/shard_map/pallas_call | solution.py:88
  120.5 48.6 %all_to_all.10 = bf16[64,64,128]{2,1,0:T(8,128)(2,1)S(1)} all-to-all(bf16[64,64,128]{2,1,0:T(8,128)(2,1)S(1)} %bitcast.41), channel_id=1, replica_groups=mesh['ylo'=4,'z'=8,'yhi'=2,'x'=4,'c'=2] {'ylo','z','c'}, dimensions={0} | all-to-all | bytes 2097152 | tf_op jit(solution)/shard_map/all_to_all | solution.py:135
  (85 shorter events, 28.8 us)
Async XLA Ops:
  3.1 111.7 %all-to-all-start = ((f32[64,8,1024]{2,1,0:T(8,128)}), f32[64,8,1024]{2,1,0:T(8,128)S(1)}, u32[]{:S(2)}, u32[]{:S(2)}) async-start(f32[64,8,1024]{2,1,0:T(8,128)} %bitcast.46), calls=%async_computation | async-start | bytes 4194304 | tf_op jit(solution)/shard_map/all_to_all | solution.py:135
  19.5 4.0 %collective-permute-start = (bf16[192,1024]{1,0:T(8,128)(2,1)}, bf16[192,1024]{1,0:T(8,128)(2,1)S(1)}, u32[]{:S(2)}, u32[]{:S(2)}) collective-permute-start(bf16[192,1024]{1,0:T(8,128)(2,1)} %get-tuple-element.37), channel_id=1, source_target_pairs={{0,1},{1,0},{2,3},{3,2},{4,5},{5,4},{6,7},{7,6},{8,9},{9,8},{10,11... | collective-permute-start | bytes 1179656 | tf_op jit(solution)/shard_map/ppermute | solution.py:129
  23.8 18.2 %collective-permute-start.7 = (bf16[3,192,512]{2,1,0:T(8,128)(2,1)S(1)}, bf16[3,192,512]{2,1,0:T(8,128)(2,1)S(1)}, u32[]{:S(2)}, u32[]{:S(2)}) collective-permute-start(bf16[3,192,512]{2,1,0:T(8,128)(2,1)S(1)} %get-tuple-element.39), channel_id=1, source_target_pairs={{0,4},{2,6},{4,0},{6,2},{1,5},{3,7},{5,1},{7,3},{8,12},{10,14},{12... | collective-permute-start | bytes 1769480 | tf_op jit(solution)/shard_map/ppermute | solution.py:132
  28.4 26.2 %collective-permute-start.9 = (bf16[3,192,512]{2,1,0:T(8,128)(2,1)S(1)}, bf16[3,192,512]{2,1,0:T(8,128)(2,1)S(1)}, u32[]{:S(2)}, u32[]{:S(2)}) collective-permute-start(bf16[3,192,512]{2,1,0:T(8,128)(2,1)S(1)} %get-tuple-element.40), channel_id=1, source_target_pairs={{0,6},{2,0},{4,2},{6,4},{1,7},{3,1},{5,3},{7,5},{8,14},{10,8},{12,... | collective-permute-start | bytes 1769480 | tf_op jit(solution)/shard_map/ppermute | solution.py:132
  31.2 31.0 %collective-permute-start.4 = (bf16[192,512]{1,0:T(8,128)(2,1)S(1)}, bf16[192,512]{1,0:T(8,128)(2,1)S(1)}, u32[]{:S(2)}, u32[]{:S(2)}) collective-permute-start(bf16[192,512]{1,0:T(8,128)(2,1)S(1)} %bitcast.49), channel_id=1, source_target_pairs={{0,1},{1,0},{2,3},{3,2},{4,5},{5,4},{6,7},{7,6},{8,9},{9,8},{10,11... | collective-permute-start | bytes 589832 | tf_op jit(solution)/shard_map/ppermute | solution.py:129
  33.9 24.4 %collective-permute-start.5 = (bf16[3,192,512]{2,1,0:T(8,128)(2,1)S(1)}, bf16[3,192,512]{2,1,0:T(8,128)(2,1)S(1)}, u32[]{:S(2)}, u32[]{:S(2)}) collective-permute-start(bf16[3,192,512]{2,1,0:T(8,128)(2,1)S(1)} %get-tuple-element.41), channel_id=1, source_target_pairs={{0,2},{2,4},{4,6},{6,0},{1,3},{3,5},{5,7},{7,1},{8,10},{10,12},{12... | collective-permute-start | bytes 1769480 | tf_op jit(solution)/shard_map/ppermute | solution.py:132
  36.6 37.5 %collective-permute-start.3 = (bf16[3,192,512]{2,1,0:T(8,128)(2,1)S(1)}, bf16[3,192,512]{2,1,0:T(8,128)(2,1)S(1)}, u32[]{:S(2)}, u32[]{:S(2)}) collective-permute-start(bf16[3,192,512]{2,1,0:T(8,128)(2,1)S(1)} %get-tuple-element.46), channel_id=1, source_target_pairs={{0,6},{2,0},{4,2},{6,4},{1,7},{3,1},{5,3},{7,5},{8,14},{10,8},{12,... | collective-permute-start | bytes 1769480 | tf_op jit(solution)/shard_map/ppermute | solution.py:132
  41.9 38.0 %copy-start = (bf16[3,192,512]{2,1,0:T(8,128)(2,1)}, bf16[3,192,512]{2,1,0:T(8,128)(2,1)S(1)}, u32[]{:S(2)}) copy-start(bf16[3,192,512]{2,1,0:T(8,128)(2,1)S(1)} %collective-permute-done.7.refs_6_.refs_10_) | copy-start | bytes 1769476
  41.9 32.3 %collective-permute-start.1 = (bf16[3,192,512]{2,1,0:T(8,128)(2,1)S(1)}, bf16[3,192,512]{2,1,0:T(8,128)(2,1)S(1)}, u32[]{:S(2)}, u32[]{:S(2)}) collective-permute-start(bf16[3,192,512]{2,1,0:T(8,128)(2,1)S(1)} %get-tuple-element.47), channel_id=1, source_target_pairs={{0,2},{2,4},{4,6},{6,0},{1,3},{3,5},{5,7},{7,1},{8,10},{10,12},{12... | collective-permute-start | bytes 1769480 | tf_op jit(solution)/shard_map/ppermute | solution.py:132
  54.7 25.3 %copy-start.2 = (bf16[3,192,512]{2,1,0:T(8,128)(2,1)}, bf16[3,192,512]{2,1,0:T(8,128)(2,1)S(1)}, u32[]{:S(2)}) copy-start(bf16[3,192,512]{2,1,0:T(8,128)(2,1)S(1)} %collective-permute-done.9.refs_7_.refs_11_) | copy-start | bytes 1769476
  54.7 25.3 %collective-permute-start.2 = (bf16[3,192,512]{2,1,0:T(8,128)(2,1)S(1)}, bf16[3,192,512]{2,1,0:T(8,128)(2,1)S(1)}, u32[]{:S(2)}, u32[]{:S(2)}) collective-permute-start(bf16[3,192,512]{2,1,0:T(8,128)(2,1)S(1)} %get-tuple-element.48), channel_id=1, source_target_pairs={{0,4},{2,6},{4,0},{6,2},{1,5},{3,7},{5,1},{7,3},{8,12},{10,14},{12... | collective-permute-start | bytes 1769480 | tf_op jit(solution)/shard_map/ppermute | solution.py:132
  58.3 21.6 %copy-start.4 = (bf16[3,192,512]{2,1,0:T(8,128)(2,1)}, bf16[3,192,512]{2,1,0:T(8,128)(2,1)S(1)}, u32[]{:S(2)}) copy-start(bf16[3,192,512]{2,1,0:T(8,128)(2,1)S(1)} %collective-permute-done.5.refs_5_.refs_9_) | copy-start | bytes 1769476
  58.3 5.8 %collective-permute-start.8 = (bf16[192,512]{1,0:T(8,128)(2,1)S(1)}, bf16[192,512]{1,0:T(8,128)(2,1)S(1)}, u32[]{:S(2)}, u32[]{:S(2)}) collective-permute-start(bf16[192,512]{1,0:T(8,128)(2,1)S(1)} %slice_bitcast_fusion.1), channel_id=1, source_target_pairs={{0,1},{1,0},{2,3},{3,2},{4,5},{5,4},{6,7},{7,6},{8,9},{9,8},{10,11... | collective-permute-start | bytes 589832 | tf_op jit(solution)/shard_map/ppermute | solution.py:129
  62.2 4.4 %collective-permute-start.10 = (bf16[192,512]{1,0:T(8,128)(2,1)S(1)}, bf16[192,512]{1,0:T(8,128)(2,1)S(1)}, u32[]{:S(2)}, u32[]{:S(2)}) collective-permute-start(bf16[192,512]{1,0:T(8,128)(2,1)S(1)} %slice_bitcast_fusion), channel_id=1, source_target_pairs={{0,1},{1,0},{2,3},{3,2},{4,5},{5,4},{6,7},{7,6},{8,9},{9,8},{10,11... | collective-permute-start | bytes 589832 | tf_op jit(solution)/shard_map/ppermute | solution.py:129
  64.1 3.5 %collective-permute-start.6 = (bf16[192,512]{1,0:T(8,128)(2,1)S(1)}, bf16[192,512]{1,0:T(8,128)(2,1)S(1)}, u32[]{:S(2)}, u32[]{:S(2)}) collective-permute-start(bf16[192,512]{1,0:T(8,128)(2,1)S(1)} %slice_bitcast_fusion.2), channel_id=1, source_target_pairs={{0,1},{1,0},{2,3},{3,2},{4,5},{5,4},{6,7},{7,6},{8,9},{9,8},{10,11... | collective-permute-start | bytes 589832 | tf_op jit(solution)/shard_map/ppermute | solution.py:129
  69.4 43.5 %collective-permute-start.17 = (bf16[512,512]{1,0:T(8,128)(2,1)}, bf16[512,512]{1,0:T(8,128)(2,1)}, u32[]{:S(2)}, u32[]{:S(2)}) collective-permute-start(bf16[512,512]{1,0:T(8,128)(2,1)} %shard_map.68), channel_id=1, source_target_pairs={{0,8},{8,0},{1,9},{9,1},{2,10},{10,2},{3,11},{11,3},{4,12},{12,4},... | collective-permute-start | bytes 1572872 | tf_op jit(solution)/shard_map/ppermute | solution.py:158
  82.7 30.3 %collective-permute-start.16 = (bf16[256,1024]{1,0:T(8,128)(2,1)}, bf16[256,1024]{1,0:T(8,128)(2,1)}, u32[]{:S(2)}, u32[]{:S(2)}) collective-permute-start(bf16[256,1024]{1,0:T(8,128)(2,1)} %constant_dynamic-slice_fusion), channel_id=1, source_target_pairs={{0,1},{1,0},{2,3},{3,2},{4,5},{5,4},{6,7},{7,6},{8,9},{9,8},{10,11... | collective-permute-start | bytes 1572872 | tf_op jit(solution)/shard_map/ppermute | solution.py:129
  86.3 7.0 %collective-permute-start.14 = (bf16[192,512]{1,0:T(8,128)(2,1)S(1)}, bf16[192,512]{1,0:T(8,128)(2,1)S(1)}, u32[]{:S(2)}, u32[]{:S(2)}) collective-permute-start(bf16[192,512]{1,0:T(8,128)(2,1)S(1)} %slice_bitcast_fusion.7), channel_id=1, source_target_pairs={{0,1},{1,0},{2,3},{3,2},{4,5},{5,4},{6,7},{7,6},{8,9},{9,8},{10,11... | collective-permute-start | bytes 589832 | tf_op jit(solution)/shard_map/ppermute | solution.py:129
  88.2 7.5 %collective-permute-start.13 = (bf16[192,512]{1,0:T(8,128)(2,1)S(1)}, bf16[192,512]{1,0:T(8,128)(2,1)S(1)}, u32[]{:S(2)}, u32[]{:S(2)}) collective-permute-start(bf16[192,512]{1,0:T(8,128)(2,1)S(1)} %slice_bitcast_fusion.8), channel_id=1, source_target_pairs={{0,1},{1,0},{2,3},{3,2},{4,5},{5,4},{6,7},{7,6},{8,9},{9,8},{10,11... | collective-permute-start | bytes 589832 | tf_op jit(solution)/shard_map/ppermute | solution.py:129
  90.6 10.5 %collective-permute-start.12 = (bf16[192,512]{1,0:T(8,128)(2,1)}, bf16[192,512]{1,0:T(8,128)(2,1)}, u32[]{:S(2)}, u32[]{:S(2)}) collective-permute-start(bf16[192,512]{1,0:T(8,128)(2,1)} %slice_bitcast_fusion.9), channel_id=1, source_target_pairs={{0,1},{1,0},{2,3},{3,2},{4,5},{5,4},{6,7},{7,6},{8,9},{9,8},{10,11... | collective-permute-start | bytes 589832 | tf_op jit(solution)/shard_map/ppermute | solution.py:129
  93.2 7.9 %collective-permute-start.11 = (bf16[192,512]{1,0:T(8,128)(2,1)}, bf16[192,512]{1,0:T(8,128)(2,1)}, u32[]{:S(2)}, u32[]{:S(2)}) collective-permute-start(bf16[192,512]{1,0:T(8,128)(2,1)} %slice_bitcast_fusion.10), channel_id=1, source_target_pairs={{0,1},{1,0},{2,3},{3,2},{4,5},{5,4},{6,7},{7,6},{8,9},{9,8},{10,11... | collective-permute-start | bytes 589832 | tf_op jit(solution)/shard_map/ppermute | solution.py:129
  96.3 21.9 %collective-permute-start.15 = (bf16[512,512]{1,0:T(8,128)(2,1)}, bf16[512,512]{1,0:T(8,128)(2,1)}, u32[]{:S(2)}, u32[]{:S(2)}) collective-permute-start(bf16[512,512]{1,0:T(8,128)(2,1)} %shard_map.69), channel_id=1, source_target_pairs={{0,8},{8,0},{1,9},{9,1},{2,10},{10,2},{3,11},{11,3},{4,12},{12,4},... | collective-permute-start | bytes 1572872 | tf_op jit(solution)/shard_map/ppermute | solution.py:158
  120.5 48.7 %copy-start.18 = (f32[1,8,2048]{2,1,0:T(8,128)S(1)}, f32[1,8,2048]{2,1,0:T(8,128)}, u32[]{:S(2)}) copy-start(f32[1,8,2048]{2,1,0:T(8,128)} %param.8) | copy-start | bytes 196612
  120.5 48.7 %copy-start.19 = (f32[1,8,2048]{2,1,0:T(8,128)S(1)}, f32[1,8,2048]{2,1,0:T(8,128)}, u32[]{:S(2)}) copy-start(f32[1,8,2048]{2,1,0:T(8,128)} %param.9) | copy-start | bytes 196612
  (18 other events, 65.2 us)
